TPU v7x, 128 devices: a whole 4x4x4 slice. The times are simulated.
128 devices in a mesh: ctx: 32 (over y, x, core), wt: 2 (over z_hi), seq: 2 (over z_lo).
Axes of the slice: x: 4, y: 4, z: 4 (z_hi: 2, z_lo: 2; z = z_hi * 2 + z_lo), core: 2. Of those that a mesh axis runs over, the one named last changes fastest.
Arguments:
- tokens: bfloat16 [4, 4096, 1536], P(('wt', 'seq'), 'ctx'), may hold values from -6 to 6
- cotangent: bfloat16 [4, 4096, 1536], P(('wt', 'seq'), 'ctx'), may hold values from -6 to 6
- segment_ids: int32 [4, 4096], P(('wt', 'seq'), 'ctx'), may hold values from 0 to 4095, as said below
- routes: int32 [4, 4096, 6], P(('wt', 'seq'), 'ctx'), may hold values from 0 to 31, all different within a row; in each aligned block of 128 rows (0 to 127, 128 to 255, ..., all dimensions but the last counted through in order) at most 48 rows name the same one
- gates: float32 [4, 4096, 6], P(('wt', 'seq'), 'ctx'), may hold values from 0.3 to 1
- dense_weights: float32 [1536, 7168], P(('ctx', 'wt', 'seq'))
- dense_first: float32 [1536, 7168], P(('ctx', 'wt', 'seq')), may hold values from -0.00015258789 to 0.00015258789
- dense_second: float32 [1536, 7168], P(('ctx', 'wt', 'seq')), may hold values from 3.2110246e-09 to 1.2844098e-08
- expert_weights: float32 [32, 1536, 1536], P('ctx', ('wt', 'seq'))
- expert_first: float32 [32, 1536, 1536], P('ctx', ('wt', 'seq')), may hold values from -3.8146973e-05 to 3.8146973e-05
- expert_second: float32 [32, 1536, 1536], P('ctx', ('wt', 'seq')), may hold values from 1.9266148e-10 to 7.7064594e-10
- gains: float32 [2, 1536], replicated
- gain_first: float32 [2, 1536], P(None, ('ctx', 'wt', 'seq')), may hold values from -0.00036621094 to 0.00036621094
- gain_second: float32 [2, 1536], P(None, ('ctx', 'wt', 'seq')), may hold values from 1.4128508e-08 to 5.7798445e-08
Outputs:
- block_out: bfloat16 [4, 4096, 1536], P(('wt', 'seq'), 'ctx')
- input_grad: float32 [4, 4096, 1536], P(('wt', 'seq'), 'ctx')
- grad_norm: float32 [], replicated
- dense_new: float32 [1536, 7168], P(('ctx', 'wt', 'seq'))
- dense_first_new: float32 [1536, 7168], P(('ctx', 'wt', 'seq'))
- dense_second_new: float32 [1536, 7168], P(('ctx', 'wt', 'seq'))
- expert_new: float32 [32, 1536, 1536], P('ctx', ('wt', 'seq'))
- expert_first_new: float32 [32, 1536, 1536], P('ctx', ('wt', 'seq'))
- expert_second_new: float32 [32, 1536, 1536], P('ctx', ('wt', 'seq'))
- gain_new: float32 [2, 1536], P(None, ('ctx', 'wt', 'seq'))
- gain_first_new: float32 [2, 1536], P(None, ('ctx', 'wt', 'seq'))
- gain_second_new: float32 [2, 1536], P(None, ('ctx', 'wt', 'seq'))
Inputs may be any that keep to these rules, and one draw needn't show every extreme that they name: `segment_ids`: document numbers start at 0 and never fall along a sequence; the last document of each sequence has the number 4096 - 1. A token's 6 experts differ; in each aligned block of 128 positions (the positions of one index of ctx) no expert is named by more than 48 routes, a bound that some block reaches.
All inputs are finite; a program needn't handle non-finite values.
Results may differ from a plain program's by a relative error of at most 0.02.
Values may be sent and summed in bfloat16 or wider, within the bound.
No kernel may reach another device: no remote copies, remote signals or barrier semaphores. Data moves between devices by JAX's collectives and lax.ppermute only.
A program may use at most 256 MiB of HBM per device.

v0:
```python
import jax
import jax.numpy as jnp
from jax import lax
from jax.sharding import PartitionSpec as P

HEADS = 12
KV_HEADS = 4
HEAD_DIM = 128
EXPERT_FF = 512
SHARED_FF = 1024
TOP = 6
EXP_DEV = 1
STEP = 10


EPS_NORM = 1e-05
CLIP_NORM = 1.0
FIRST_DECAY = 0.9
SECOND_DECAY = 0.95
ADAM_EPS = 1e-08
WEIGHT_DECAY = 0.1
MATRIX_RATE = 0.05
GAIN_RATE = 0.6
NEGATIVE = -1e30


def sent_to_all(array, axis):
    count = lax.axis_size(axis)
    return lax.all_to_all(
        jnp.broadcast_to(array[None], (count, *array.shape)), axis, 0, 0, tiled=True
    )


def in_order(blocks, dim):
    lengths = list(blocks.shape[1:])
    lengths[dim] *= blocks.shape[0]
    return jnp.moveaxis(blocks, 0, dim).reshape(lengths)


def collect(array, axis, dim):
    blocks = sent_to_all(array, axis)
    return in_order(blocks, dim)


def side_by_side(arrays, axis, dim, along):
    widths = [a.shape[along] for a in arrays]
    both = jnp.concatenate(arrays, axis=along)
    filled = lax.all_gather(both, axis, axis=dim, tiled=True)
    return tuple(jnp.split(filled, [sum(widths[:k]) for k in range(1, len(widths))], axis=along))


def side_by_side_2(arrays, axis, dim, along):
    ends, at = ([], 0)
    for a in arrays[:-1]:
        at += a.shape[along]
        ends.append(at)
    both = jnp.concatenate(arrays, axis=along)
    return tuple(
        jnp.split(lax.psum_scatter(both, axis, scatter_dimension=dim, tiled=True), ends, axis=along)
    )


def in_blocks(array, dim, count):
    lengths = array.shape
    blocks = array.reshape(*lengths[:dim], count, lengths[dim] // count, *lengths[dim + 1 :])
    return jnp.moveaxis(blocks, dim, 0)


def sent_and_summed(array, axis, dim):
    count = lax.axis_size(axis)
    blocks = lax.all_to_all(in_blocks(array, dim, count), axis, 0, 0, tiled=True)
    return jnp.sum(blocks.astype(jnp.float32), axis=0)


def gathered_total(array, axis):
    return lax.all_gather(array, axis).sum(0)


def silu_parts(values):
    sigmoid_values = jax.nn.sigmoid(values)
    return (values * sigmoid_values, sigmoid_values * (1.0 + values * (1.0 - sigmoid_values)))


def norm_forward(values, gain_row):
    factor = lax.rsqrt(jnp.mean(values * values, axis=-1, keepdims=True) + EPS_NORM)
    normed = values * factor
    return (normed * gain_row, normed, factor)


def norm_backward(upstream, normed, factor, gain_row):
    scaled = upstream * gain_row
    inward = factor * (scaled - normed * jnp.mean(scaled * normed, axis=-1, keepdims=True))
    return (inward, jnp.sum(upstream * normed, axis=0))


def adamw_step(weight, first_moment, second, gradient, step_rate, decay_rate):
    first_moment = FIRST_DECAY * first_moment + (1.0 - FIRST_DECAY) * gradient
    second = SECOND_DECAY * second + (1.0 - SECOND_DECAY) * gradient * gradient
    first_hat = first_moment / (1.0 - FIRST_DECAY**STEP)
    second_hat = second / (1.0 - SECOND_DECAY**STEP)
    weight = weight - step_rate * (
        first_hat / (jnp.sqrt(second_hat) + ADAM_EPS) + decay_rate * weight
    )
    return (weight, first_moment, second)


def times_transposed(left, right):
    return lax.dot_general(
        left, right, (((1,), (1,)), ((), ())), preferred_element_type=jnp.float32
    )


def transposed_times(left, right):
    return lax.dot_general(
        left, right, (((0,), (0,)), ((), ())), preferred_element_type=jnp.float32
    )


def head_scores(query_head, key_head, visible, scale_factor):
    scores = (
        jnp.einsum("qgd,sd->gqs", query_head, key_head, preferred_element_type=jnp.float32)
        * scale_factor
    )
    return jnp.where(visible[None], scores, NEGATIVE)


def shards(
    tokens,
    cotangent,
    segment_ids,
    routes,
    gates,
    dense_weights,
    dense_first,
    dense_second,
    expert_weights,
    expert_first,
    expert_second,
    gains,
    gain_first,
    gain_second,
):
    tok_rows = tokens.shape[1]
    model_width = tokens.shape[2]
    ctx_count = lax.axis_size("ctx")
    expert_count = EXP_DEV * ctx_count
    capacity = min(tok_rows, 2 * tok_rows * TOP // expert_count)
    seq_len = tok_rows * ctx_count
    query_width = HEADS * HEAD_DIM
    kv_width = KV_HEADS * HEAD_DIM
    group_size = HEADS // KV_HEADS
    group_width = group_size * HEAD_DIM
    qkv_end = query_width + 2 * kv_width
    shared_start = qkv_end + query_width
    down_start = shared_start + 2 * SHARED_FF
    scale_factor = HEAD_DIM ** (-0.5)
    dense_low = dense_weights.astype(jnp.bfloat16)
    expert_low = expert_weights.astype(jnp.bfloat16)
    dense_all = lax.all_gather(dense_low, ("ctx", "wt", "seq"), axis=0, tiled=True)
    inputs = tokens[0].astype(jnp.float32)
    h_one_f, normed_one, factor_one = norm_forward(inputs, gains[0])
    h_one = h_one_f.astype(jnp.bfloat16)
    projected = jnp.dot(h_one, dense_all[:, :qkv_end], preferred_element_type=jnp.float32)
    query = projected[:, :query_width].astype(jnp.bfloat16)
    key_own = projected[:, query_width : query_width + kv_width].astype(jnp.bfloat16)
    value_own = projected[:, query_width + kv_width :].astype(jnp.bfloat16)
    segments_all = collect(segment_ids, "ctx", 1)[0]
    keys_all, values_all = side_by_side((key_own, value_own), "ctx", 0, 1)
    first_spot = lax.axis_index("ctx") * tok_rows
    query_spots = first_spot + jnp.arange(tok_rows, dtype=jnp.int32)
    key_spots = jnp.arange(seq_len, dtype=jnp.int32)
    visible = (segment_ids[0][:, None] == segments_all[None, :]) & (
        key_spots[None, :] <= query_spots[:, None]
    )
    head_outputs = []
    log_totals = []
    for kv_head in range(KV_HEADS):
        query_head = query[:, kv_head * group_width : (kv_head + 1) * group_width].reshape(
            tok_rows, group_size, HEAD_DIM
        )
        key_head = keys_all[:, kv_head * HEAD_DIM : (kv_head + 1) * HEAD_DIM]
        value_head = values_all[:, kv_head * HEAD_DIM : (kv_head + 1) * HEAD_DIM]
        scores = head_scores(query_head, key_head, visible, scale_factor)
        highest = jnp.max(scores, axis=-1, keepdims=True)
        expo_scores = jnp.exp(scores - highest)
        totals = jnp.sum(expo_scores, axis=-1, keepdims=True)
        weights_low = (expo_scores / totals).astype(jnp.bfloat16)
        head_result = jnp.einsum(
            "gqs,sd->qgd", weights_low, value_head, preferred_element_type=jnp.float32
        )
        head_outputs.append(head_result.reshape(tok_rows, group_width))
        log_totals.append(highest + jnp.log(totals))
    attn = jnp.concatenate(head_outputs, axis=1).astype(jnp.bfloat16)
    resid = inputs + times_transposed(attn, dense_all[:, qkv_end:shared_start])
    h_two_f, normed_two, factor_two = norm_forward(resid, gains[1])
    h_two = h_two_f.astype(jnp.bfloat16)
    shared_pre = jnp.dot(
        h_two, dense_all[:, shared_start:down_start], preferred_element_type=jnp.float32
    )
    shared_gate = shared_pre[:, :SHARED_FF]
    shared_up = shared_pre[:, SHARED_FF:]
    shared_act, shared_deriv = silu_parts(shared_gate)
    shared_mid = (shared_act * shared_up).astype(jnp.bfloat16)
    shared_out = times_transposed(shared_mid, dense_all[:, down_start:])
    route_flat = routes[0].reshape(-1)
    labels = jnp.arange(expert_count, dtype=jnp.int32)
    onehot = (route_flat[:, None] == labels[None, :]).astype(jnp.int32)
    slot_flat = jnp.sum((jnp.cumsum(onehot, axis=0) - onehot) * onehot, axis=1)
    token_flat = jnp.arange(tok_rows * TOP, dtype=jnp.int32) // TOP
    outgoing = (
        jnp.zeros((expert_count, capacity, model_width), jnp.bfloat16)
        .at[route_flat, slot_flat]
        .set(h_two[token_flat])
    )
    arrived = lax.all_to_all(outgoing, "ctx", split_axis=0, concat_axis=0, tiled=True).reshape(
        ctx_count, EXP_DEV, capacity, model_width
    )
    expert_all = lax.all_gather(expert_low, ("wt", "seq"), axis=1, tiled=True)
    expert_pre = jnp.einsum(
        "sjcd,jdf->sjcf",
        arrived,
        expert_all[:, :, : 2 * EXPERT_FF],
        preferred_element_type=jnp.float32,
    )
    expert_gate = expert_pre[..., :EXPERT_FF]
    expert_up = expert_pre[..., EXPERT_FF:]
    expert_act, expert_deriv = silu_parts(expert_gate)
    expert_mid = (expert_act * expert_up).astype(jnp.bfloat16)
    expert_out = jnp.einsum(
        "sjcf,jdf->sjcd",
        expert_mid,
        expert_all[:, :, 2 * EXPERT_FF :],
        preferred_element_type=jnp.float32,
    ).astype(jnp.bfloat16)
    returned = lax.all_to_all(
        expert_out.reshape(expert_count, capacity, model_width),
        "ctx",
        split_axis=0,
        concat_axis=0,
        tiled=True,
    )
    gate_rows = gates[0]
    picked = returned[route_flat, slot_flat].astype(jnp.float32).reshape(tok_rows, TOP, model_width)
    mixture = jnp.sum(gate_rows[:, :, None] * picked, axis=1)
    block_out = (resid + shared_out + mixture).astype(jnp.bfloat16)
    upstream = cotangent[0]
    upstream_f = upstream.astype(jnp.float32)
    toward = (
        (gate_rows[:, :, None] * upstream_f[:, None, :])
        .astype(jnp.bfloat16)
        .reshape(tok_rows * TOP, model_width)
    )
    grad_outgoing = (
        jnp.zeros((expert_count, capacity, model_width), jnp.bfloat16)
        .at[route_flat, slot_flat]
        .set(toward)
    )
    grad_arrived = lax.all_to_all(
        grad_outgoing, "ctx", split_axis=0, concat_axis=0, tiled=True
    ).reshape(ctx_count, EXP_DEV, capacity, model_width)
    dense_all = lax.all_gather(dense_low, ("ctx", "wt", "seq"), axis=0, tiled=True)
    expert_all = lax.all_gather(expert_low, ("wt", "seq"), axis=1, tiled=True)
    grad_down = jnp.einsum(
        "sjcd,sjcf->jdf", grad_arrived, expert_mid, preferred_element_type=jnp.float32
    )
    grad_mid = jnp.einsum(
        "sjcd,jdf->sjcf",
        grad_arrived,
        expert_all[:, :, 2 * EXPERT_FF :],
        preferred_element_type=jnp.float32,
    )
    grad_gate = (grad_mid * expert_up * expert_deriv).astype(jnp.bfloat16)
    grad_up = (grad_mid * expert_act).astype(jnp.bfloat16)
    grad_both = jnp.concatenate([grad_gate, grad_up], axis=-1)
    grad_pre_weights = jnp.einsum(
        "sjcd,sjcf->jdf", arrived, grad_both, preferred_element_type=jnp.float32
    )
    grad_rows = jnp.einsum(
        "sjcf,jdf->sjcd",
        grad_both,
        expert_all[:, :, : 2 * EXPERT_FF],
        preferred_element_type=jnp.float32,
    )
    expert_local = jnp.concatenate([grad_pre_weights, grad_down], axis=-1)
    expert_grad = lax.psum_scatter(
        expert_local.astype(jnp.bfloat16), ("wt", "seq"), scatter_dimension=1, tiled=True
    ).astype(jnp.float32)
    back_rows = lax.all_to_all(
        grad_rows.reshape(expert_count, capacity, model_width).astype(jnp.bfloat16),
        "ctx",
        split_axis=0,
        concat_axis=0,
        tiled=True,
    ).astype(jnp.float32)
    grad_h_experts = jnp.sum(
        back_rows[route_flat, slot_flat].reshape(tok_rows, TOP, model_width), axis=1
    )
    grad_shared_mid = jnp.dot(
        upstream, dense_all[:, down_start:], preferred_element_type=jnp.float32
    )
    grad_shared_gate = (grad_shared_mid * shared_up * shared_deriv).astype(jnp.bfloat16)
    grad_shared_up = (grad_shared_mid * shared_act).astype(jnp.bfloat16)
    grad_shared = jnp.concatenate([grad_shared_gate, grad_shared_up], axis=1)
    grad_h_two = (
        times_transposed(grad_shared, dense_all[:, shared_start:down_start]) + grad_h_experts
    )
    grad_resid_norm, gain_two_part = norm_backward(grad_h_two, normed_two, factor_two, gains[1])
    grad_resid = upstream_f + grad_resid_norm
    grad_att = grad_resid.astype(jnp.bfloat16)
    grad_attn = jnp.dot(
        grad_att, dense_all[:, qkv_end:shared_start], preferred_element_type=jnp.float32
    ).astype(jnp.bfloat16)
    query_grads = []
    key_grads = []
    value_grads = []
    for kv_head in range(KV_HEADS):
        query_head = query[:, kv_head * group_width : (kv_head + 1) * group_width].reshape(
            tok_rows, group_size, HEAD_DIM
        )
        key_head = keys_all[:, kv_head * HEAD_DIM : (kv_head + 1) * HEAD_DIM]
        value_head = values_all[:, kv_head * HEAD_DIM : (kv_head + 1) * HEAD_DIM]
        grad_head = grad_attn[:, kv_head * group_width : (kv_head + 1) * group_width].reshape(
            tok_rows, group_size, HEAD_DIM
        )
        scores = head_scores(query_head, key_head, visible, scale_factor)
        chances = jnp.exp(scores - log_totals[kv_head])
        grad_chances = jnp.einsum(
            "qgd,sd->gqs", grad_head, value_head, preferred_element_type=jnp.float32
        )
        centre = jnp.sum(chances * grad_chances, axis=-1, keepdims=True)
        grad_scores = (chances * (grad_chances - centre)).astype(jnp.bfloat16)
        query_grad = (
            jnp.einsum("gqs,sd->qgd", grad_scores, key_head, preferred_element_type=jnp.float32)
            * scale_factor
        )
        key_grad = (
            jnp.einsum("gqs,qgd->sd", grad_scores, query_head, preferred_element_type=jnp.float32)
            * scale_factor
        )
        value_grad = jnp.einsum(
            "gqs,qgd->sd",
            chances.astype(jnp.bfloat16),
            grad_head,
            preferred_element_type=jnp.float32,
        )
        query_grads.append(query_grad.reshape(tok_rows, group_width))
        key_grads.append(key_grad)
        value_grads.append(value_grad)
    grad_query = jnp.concatenate(query_grads, axis=1).astype(jnp.bfloat16)
    key_terms = jnp.concatenate(key_grads, axis=1)
    value_terms = jnp.concatenate(value_grads, axis=1)
    grad_keys, grad_values = tuple(
        (
            part.astype(jnp.float32)
            for part in side_by_side_2(
                (key_terms.astype(jnp.bfloat16), value_terms.astype(jnp.bfloat16)), "ctx", 0, 1
            )
        )
    )
    grad_qkv = jnp.concatenate(
        [grad_query, grad_keys.astype(jnp.bfloat16), grad_values.astype(jnp.bfloat16)], axis=1
    )
    grad_h_one = times_transposed(grad_qkv, dense_all[:, :qkv_end])
    grad_input_norm, gain_one_part = norm_backward(grad_h_one, normed_one, factor_one, gains[0])
    input_grad = grad_resid + grad_input_norm

    def product(left, right):
        return transposed_times(left, right)

    cycle_part = lax.psum_scatter(
        jnp.concatenate(
            [
                product(h_one, grad_qkv),
                product(grad_att, attn),
                product(h_two, grad_shared),
                product(upstream, shared_mid),
            ],
            axis=1,
        ).astype(jnp.bfloat16),
        "ctx",
        scatter_dimension=0,
        tiled=True,
    )
    dense_grad = sent_and_summed(cycle_part, ("wt", "seq"), 0)
    gain_part = jnp.stack([gain_one_part, gain_two_part])
    local_squares = jnp.sum(dense_grad * dense_grad) + jnp.sum(expert_grad * expert_grad)
    gain_grad, total_squares = (
        gathered_total(gain_part, ("ctx", "wt", "seq")),
        gathered_total(local_squares, ("ctx", "wt", "seq")),
    )
    grad_norm = jnp.sqrt(total_squares + jnp.sum(gain_grad * gain_grad))
    clip_factor = jnp.minimum(1.0, CLIP_NORM / (grad_norm + 1e-06))
    dense_new, dense_first_new, dense_second_new = adamw_step(
        dense_weights,
        dense_first,
        dense_second,
        dense_grad * clip_factor,
        MATRIX_RATE,
        WEIGHT_DECAY,
    )
    expert_new, expert_first_new, expert_second_new = adamw_step(
        expert_weights,
        expert_first,
        expert_second,
        expert_grad * clip_factor,
        MATRIX_RATE,
        WEIGHT_DECAY,
    )
    gain_cols = gain_first.shape[1]
    gain_begin = lax.axis_index(("ctx", "wt", "seq")) * gain_cols
    gain_slice = lax.dynamic_slice_in_dim(gains, gain_begin, gain_cols, 1)
    gain_grad_slice = lax.dynamic_slice_in_dim(gain_grad, gain_begin, gain_cols, 1)
    gain_new, gain_first_new, gain_second_new = adamw_step(
        gain_slice, gain_first, gain_second, gain_grad_slice * clip_factor, GAIN_RATE, 0.0
    )
    return (
        block_out[None],
        input_grad[None],
        grad_norm,
        dense_new,
        dense_first_new,
        dense_second_new,
        expert_new,
        expert_first_new,
        expert_second_new,
        gain_new,
        gain_first_new,
        gain_second_new,
    )


def solution(mesh):
    return jax.shard_map(
        shards,
        mesh=mesh,
        in_specs=(
            P(("wt", "seq"), "ctx", None),
            P(("wt", "seq"), "ctx", None),
            P(("wt", "seq"), "ctx"),
            P(("wt", "seq"), "ctx", None),
            P(("wt", "seq"), "ctx", None),
            P(("ctx", "wt", "seq"), None),
            P(("ctx", "wt", "seq"), None),
            P(("ctx", "wt", "seq"), None),
            P("ctx", ("wt", "seq"), None),
            P("ctx", ("wt", "seq"), None),
            P("ctx", ("wt", "seq"), None),
            P(),
            P(None, ("ctx", "wt", "seq")),
            P(None, ("ctx", "wt", "seq")),
        ),
        out_specs=(
            P(("wt", "seq"), "ctx", None),
            P(("wt", "seq"), "ctx", None),
            P(),
            P(("ctx", "wt", "seq"), None),
            P(("ctx", "wt", "seq"), None),
            P(("ctx", "wt", "seq"), None),
            P("ctx", ("wt", "seq"), None),
            P("ctx", ("wt", "seq"), None),
            P("ctx", ("wt", "seq"), None),
            P(None, ("ctx", "wt", "seq")),
            P(None, ("ctx", "wt", "seq")),
            P(None, ("ctx", "wt", "seq")),
        ),
        check_vma=False,
    )
```

profile of v0, /device:TPU:0, one launch (start us, length us, event | category | flops | bytes accessed | tf_op | source)
XLA Modules:
  0.0 1206.3 jit_solution(5806989915733458515)
XLA Ops:
  11.9 103.1 %all-gather.12.cloned.1.call-done = bf16[128,12,7168]{2,1,0:T(8,128)(2,1)} async-done(((bf16[1,12,7168]{2,1,0:T(8,128)(2,1)}), bf16[128,12,7168]{2,1,0:T(8,128)(2,1)}) %all-gather.12.cloned.1.call-update) | async-done | bytes 22020112 | tf_op jit(solution)/shard_map/all_gather | solution.py:159
  115.0 30.9 %reshape.468 = bf16[1536,7168]{1,0:T(8,128)(2,1)} reshape(bf16[128,12,7168]{2,1,0:T(8,128)(2,1)} %all-gather.12.cloned.1.call-done) | data formatting | bytes 44040192
  146.0 4.5 fusion.52
  151.9 7.1 all-to-all-start
  169.3 34.3 %all-gather.8.cloned.1.call-done = bf16[4096,1024]{1,0:T(8,128)(2,1)} async-done(((bf16[128,1024]{1,0:T(8,128)(2,1)}), bf16[4096,1024]{1,0:T(8,128)(2,1)}) %all-gather.8.cloned.1.call-update) | async-done | bytes 8388624 | tf_op jit(solution)/shard_map/all_gather | solution.py:48
  231.3 119.7 %scatter_fusion = bf16[32,48,1536]{2,1,0:T(8,128)(2,1)} fusion(bf16[32,48,1536]{2,1,0:T(8,128)(2,1)} %broadcast.265.clone, s32[768]{0:T(1024)S(1)} %get-tuple-element.55, bf16[768,1536]{1,0:T(8,128)(2,1)S(1)} %gather_fusion), kind=kCustom, calls=%fused_computation.3 | custom fusion | bytes 7084032 | tf_op jit(solution)/shard_map/scatter | solution.py:213
  351.0 5.8 all-to-all-start.1
  362.6 6.5 mul.406
  376.3 119.9 %scatter_fusion.1 = bf16[32,48,1536]{2,1,0:T(8,128)(2,1)} fusion(bf16[32,48,1536]{2,1,0:T(8,128)(2,1)} %broadcast.265.clone.1, s32[768]{0:T(1024)S(1)} %get-tuple-element.55, bf16[768,1536]{1,0:T(8,128)(2,1)S(1)} %multiply_convert_fusion), kind=kCustom, calls=%fused_computation.4 | custom fusion | bytes 7084032 | tf_op jit(solution)/shard_map/scatter | solution.py:256
  496.3 7.6 all-to-all-start.3
  503.9 9.9 fusion.81
  513.8 49.8 %all-to-all-done.3 = bf16[32,48,1536]{2,1,0:T(8,128)(2,1)} async-done(((bf16[32,48,1536]{2,1,0:T(8,128)(2,1)}), bf16[32,48,1536]{2,1,0:T(8,128)(2,1)}, u32[]{:S(2)}, u32[]{:S(2)}) %all-to-all-start.3) | async-done | bytes 4718624 | tf_op jit(solution)/shard_map/all_to_all | solution.py:258
  563.6 9.8 fusion.62
  574.5 7.0 convolution_convert_fusion.3
  581.5 4.9 all-to-all-start.4
  594.0 52.1 %all-to-all-done.4 = bf16[32,48,1536]{2,1,0:T(8,128)(2,1)} async-done(((bf16[32,48,1536]{2,1,0:T(8,128)(2,1)}), bf16[32,48,1536]{2,1,0:T(8,128)(2,1)}, u32[]{:S(2)}, u32[]{:S(2)}) %all-to-all-start.4) | async-done | bytes 4718624 | tf_op jit(solution)/shard_map/all_to_all | solution.py:288
  646.2 7.4 convert_element_type.170
  653.5 13.3 %gather_fusion.2 = f32[768,1536]{1,0:T(8,128)} fusion(f32[32,48,1536]{2,1,0:T(8,128)} %convert_element_type.170, s32[768]{0:T(1024)S(1)} %get-tuple-element.54), kind=kCustom, calls=%fused_computation.2 | custom fusion | bytes 9443328 | tf_op jit(solution)/shard_map/gather | solution.py:296
  666.8 6.6 reshape.420
  673.4 4.7 reduce_sum.218
  678.1 6.0 multiply_reduce_fusion.1
  688.3 4.6 fusion.13
  699.5 5.8 fusion.10
  705.3 6.0 fusion.12
  711.4 6.1 fusion.7
  717.5 6.1 fusion.9
  723.6 5.1 fusion.4
  728.8 6.0 fusion.6
  752.2 11.9 copy.229
  765.6 5.2 fusion.80
  770.8 8.1 fusion.56
  781.4 23.2 %copy.231 = bf16[1,1536,1536]{2,0,1:T(2,128)(2,1)} copy(bf16[1,1536,1536]{1,2,0:T(8,128)(2,1)} %pad_maximum_fusion.1) | data formatting | bytes 9437184
  804.6 7.3 copy.237
  815.1 4.5 convolution_convert_fusion.1
  834.1 19.1 %reduce-scatter.10.cloned.1.call-done = bf16[128,1024]{1,0:T(8,128)(2,1)} async-done(((bf16[4096,1024]{1,0:T(8,128)(2,1)}), bf16[128,1024]{1,0:T(8,128)(2,1)}) %reduce-scatter.10.cloned.1.call-update) | async-done | bytes 262160
  858.5 13.2 %pad_maximum_fusion = bf16[1536,7168]{1,0:T(8,128)(2,1)} fusion(bf16[1536,1024]{1,0:T(8,128)(2,1)} %fusion.55, bf16[1536,2048]{1,0:T(8,128)(2,1)} %convolution_convert_fusion.1, bf16[1536,1536]{1,0:T(8,128)(2,1)} %convolution_convert_fusion.2, bf16[1536,2560]{1,0:T(8,128)(2,1)S(1)} %convolution_convert_fusion), kind=kLoop, calls=%fused_computation.5 | loop fusion | flops 88080384 | bytes 44040192 | tf_op jit(solution)/shard_map/concatenate | solution.py:371
  873.1 5.7 convolution_convert_fusion.4
  878.9 5.5 all-to-all-start.2
  884.7 7.8 fusion.131
  900.3 43.9 %all-to-all-done.2 = bf16[32,48,1536]{2,1,0:T(8,128)(2,1)} async-done(((bf16[32,48,1536]{2,1,0:T(8,128)(2,1)}), bf16[32,48,1536]{2,1,0:T(8,128)(2,1)}, u32[]{:S(2)}, u32[]{:S(2)}) %all-to-all-start.2) | async-done | bytes 4718624 | tf_op jit(solution)/shard_map/all_to_all | solution.py:235
  944.2 11.7 gather_fusion.1
  959.1 5.2 multiply_reduce_fusion
  972.3 5.6 copy.232
  979.1 62.3 %reduce-scatter.8.cloned.1.call-done = bf16[48,7168]{1,0:T(8,128)(2,1)} async-done(((bf16[1536,7168]{1,0:T(8,128)(2,1)}), bf16[48,7168]{1,0:T(8,128)(2,1)}) %reduce-scatter.8.cloned.1.call-update) | async-done | bytes 688144 | tf_op jit(solution)/shard_map/reduce_scatter | solution.py:370
  1043.6 4.6 all-to-all-start.5
  1050.6 57.5 %all-gather.14.cloned.1.call-done = f32[128,2,1536]{2,1,0:T(2,128)} async-done(((f32[1,2,1536]{2,1,0:T(2,128)}), f32[128,2,1536]{2,1,0:T(2,128)}) %all-gather.14.cloned.1.call-update) | async-done | bytes 1572880 | tf_op jit(solution)/shard_map/all_gather | solution.py:76
  1113.7 62.7 %all-reduce = f32[128]{0:T(128)S(1)} all-reduce(f32[128]{0:T(128)S(1)} %dynamic-update-slice), channel_id=1, replica_groups=mesh['ctx'=32,'wt'=2,'seq'=2] {'ctx','wt','seq'}, use_global_device_ids=true, to_apply=%add | all-reduce | flops 128 | bytes 1024
  1178.3 7.2 multiply_subtract_fusion
  (322 shorter events, 162.4 us)
Async XLA Ops:
  8.0 107.0 %all-gather.12.cloned.1.call-start = ((), (), s32[]{:S(2)}) async-start(), calls=%async_computation.12 | async-start | bytes 29589504 | tf_op jit(solution)/shard_map/all_gather | solution.py:159
  9.8 193.7 %all-gather.8.cloned.1.call-start = ((), (), s32[]{:S(2)}) async-start(), calls=%async_computation.9 | async-start | bytes 8650752 | tf_op jit(solution)/shard_map/all_gather | solution.py:48
  10.7 135.3 %copy-start.29 = (f32[1536]{0:T(1024)}, f32[1536]{0:T(1024)S(1)}, u32[]{:S(2)}) copy-start(f32[1536]{0:T(1024)S(1)} %get-tuple-element.53) | copy-start | bytes 18436
  11.9 134.1 %copy-start.64 = (f32[128]{0:T(128)}, f32[128]{0:T(128)S(1)}, u32[]{:S(2)}) copy-start(f32[128]{0:T(128)S(1)} %add_rsqrt_fusion.1) | copy-start | bytes 1540
  11.9 134.1 %copy-start.10 = (bf16[1,128,1536]{2,1,0:T(8,128)(2,1)S(1)}, bf16[1,128,1536]{2,1,0:T(8,128)(2,1)}, u32[]{:S(2)}) copy-start(bf16[1,128,1536]{2,1,0:T(8,128)(2,1)} %param.14) | copy-start | bytes 1179652
  146.0 13.0 %copy-start.66 = (s32[1,128,6]{1,0,2:T(1,128)S(1)}, s32[1,128,6]{1,0,2:T(1,128)}, u32[]{:S(2)}) copy-start(s32[1,128,6]{1,0,2:T(1,128)} %param.17) | copy-start | bytes 9220
  151.9 14.4 %all-to-all-start = ((s32[32,1,128]{2,1,0:T(1,128)}), s32[32,1,128]{2,1,0:T(1,128)S(1)}, u32[]{:S(2)}, u32[]{:S(2)}) async-start(s32[32,1,128]{2,1,0:T(1,128)} %broadcast_in_dim.46), calls=%async_computation | async-start | bytes 32768 | tf_op jit(solution)/shard_map/all_to_all | solution.py:29
  168.8 38.2 %copy-start.39 = (bf16[128,384]{0,1:T(8,128)(2,1)}, bf16[128,384]{0,1:T(8,128)(2,1)S(1)}, u32[]{:S(2)}) copy-start(bf16[128,384]{0,1:T(8,128)(2,1)S(1)} %copy.143) | copy-start | bytes 294916
  169.0 38.1 %copy-start.41 = (bf16[128,384]{0,1:T(8,128)(2,1)}, bf16[128,384]{0,1:T(8,128)(2,1)S(1)}, u32[]{:S(2)}) copy-start(bf16[128,384]{0,1:T(8,128)(2,1)S(1)} %copy.139) | copy-start | bytes 294916
  169.1 40.7 %copy-start.43 = (bf16[128,384]{0,1:T(8,128)(2,1)}, bf16[128,384]{0,1:T(8,128)(2,1)S(1)}, u32[]{:S(2)}) copy-start(bf16[128,384]{0,1:T(8,128)(2,1)S(1)} %copy.135) | copy-start | bytes 294916
  169.3 42.8 %copy-start.45 = (bf16[128,384]{0,1:T(8,128)(2,1)}, bf16[128,384]{0,1:T(8,128)(2,1)S(1)}, u32[]{:S(2)}) copy-start(bf16[128,384]{0,1:T(8,128)(2,1)S(1)} %copy.131) | copy-start | bytes 294916
  206.2 8.1 copy-start
  206.2 8.1 copy-start.47
  224.7 459.3 %copy-start.8 = (f32[128,1536]{1,0:T(8,128)}, f32[128,1536]{1,0:T(8,128)S(1)}, u32[]{:S(2)}) copy-start(f32[128,1536]{1,0:T(8,128)S(1)} %get-tuple-element.88) | copy-start | bytes 2359300
  351.0 145.3 %all-to-all-start.1 = ((bf16[32,48,1536]{2,1,0:T(8,128)(2,1)}), bf16[32,48,1536]{2,1,0:T(8,128)(2,1)}, u32[]{:S(2)}, u32[]{:S(2)}) async-start(bf16[32,48,1536]{2,1,0:T(8,128)(2,1)} %scatter_fusion), calls=%async_computation.1 | async-start | bytes 9437184 | tf_op jit(solution)/shard_map/all_to_all | solution.py:215
  356.8 147.2 %all-gather.10.cloned.1.call-start = ((), (), s32[]{:S(2)}) async-start(), calls=%async_computation.10 | async-start | bytes 5898240 | tf_op jit(solution)/shard_map/all_gather | solution.py:218
  496.3 67.3 %all-to-all-start.3 = ((bf16[32,48,1536]{2,1,0:T(8,128)(2,1)}), bf16[32,48,1536]{2,1,0:T(8,128)(2,1)}, u32[]{:S(2)}, u32[]{:S(2)}) async-start(bf16[32,48,1536]{2,1,0:T(8,128)(2,1)} %scatter_fusion.1), calls=%async_computation.3 | async-start | bytes 9437184 | tf_op jit(solution)/shard_map/all_to_all | solution.py:258
  563.6 10.9 copy-start.73
  573.4 8.1 copy-start.77
  581.5 64.6 %all-to-all-start.4 = ((bf16[32,48,1536]{2,1,0:T(8,128)(2,1)}), bf16[32,48,1536]{2,1,0:T(8,128)(2,1)}, u32[]{:S(2)}, u32[]{:S(2)}) async-start(bf16[32,48,1536]{2,1,0:T(8,128)(2,1)} %convolution_convert_fusion.3), calls=%async_computation.4 | async-start | bytes 9437184 | tf_op jit(solution)/shard_map/all_to_all | solution.py:288
  586.4 266.7 %reduce-scatter.10.cloned.1.call-start = ((), (), s32[]{:S(2)}) async-start(), calls=%async_computation.14 | async-start | bytes 8650752
  594.0 218.4 %copy-start.23 = (bf16[128,1024]{1,0:T(8,128)(2,1)}, bf16[128,1024]{1,0:T(8,128)(2,1)S(1)}, u32[]{:S(2)}) copy-start(bf16[128,1024]{1,0:T(8,128)(2,1)S(1)} %get-tuple-element.70) | copy-start | bytes 786436
  684.3 146.2 %copy-start.4 = (f32[128,1536]{1,0:T(8,128)}, f32[128,1536]{1,0:T(8,128)S(1)}, u32[]{:S(2)}) copy-start(f32[128,1536]{1,0:T(8,128)S(1)} %multiply_add_fusion) | copy-start | bytes 2359300
  688.3 11.2 slice-start.4
  697.4 13.9 %slice-start.2 = ((s8[6291456]{0:T(1024)(128)(4,1)}), s8[4194304]{0:T(1024)(128)(4,1)S(1)}, s32[]{:S(2)}) async-start(s8[6291456]{0:T(1024)(128)(4,1)} %bitcast.341), calls=%async_computation.18 | async-start | bytes 8388608
  699.5 11.8 slice-start.3
  705.3 18.3 %slice-start = ((s8[6291456]{0:T(1024)(128)(4,1)}), s8[4194304]{0:T(1024)(128)(4,1)S(1)}, s32[]{:S(2)}) async-start(s8[6291456]{0:T(1024)(128)(4,1)} %bitcast.339), calls=%async_computation.16 | async-start | bytes 8388608
  711.3 23.4 %copy-start.17 = (bf16[3,128,4096]{1,2,0:T(8,128)(2,1)}, bf16[3,128,4096]{1,2,0:T(8,128)(2,1)S(1)}, u32[]{:S(2)}) copy-start(bf16[3,128,4096]{1,2,0:T(8,128)(2,1)S(1)} %fusion.12) | copy-start | bytes 9437188
  711.4 12.3 %slice-start.1 = ((s8[6291456]{0:T(1024)(128)(4,1)}), s8[2097152]{0:T(1024)(128)(4,1)S(1)}, s32[]{:S(2)}) async-start(s8[6291456]{0:T(1024)(128)(4,1)} %bitcast.339), calls=%async_computation.17 | async-start | bytes 4194304
  728.8 8.1 copy-start.42
  734.8 8.7 slice-start.8
  736.9 8.7 slice-start.6
  764.2 204.1 %reduce-scatter.12.cloned.1.call-start = ((), (), s32[]{:S(2)}) async-start(), calls=%async_computation.15 | async-start | bytes 5898240
  812.0 229.4 %reduce-scatter.8.cloned.1.call-start = ((), (), s32[]{:S(2)}) async-start(), calls=%async_computation.11 | async-start | bytes 22708224 | tf_op jit(solution)/shard_map/reduce_scatter | solution.py:370
  819.7 8.2 copy-start.21
  822.5 8.1 copy-start.38
  829.9 25.2 %copy-start.11 = (bf16[1,128,1536]{2,1,0:T(8,128)(2,1)S(1)}, bf16[1,128,1536]{2,1,0:T(8,128)(2,1)}, u32[]{:S(2)}) copy-start(bf16[1,128,1536]{2,1,0:T(8,128)(2,1)} %param.14) | copy-start | bytes 1179652
  829.9 25.2 %copy-start.30 = (f32[1536]{0:T(1024)S(1)}, f32[1536]{0:T(1024)}, u32[]{:S(2)}) copy-start(f32[1536]{0:T(1024)} %copy-done.29) | copy-start | bytes 18436
  829.9 25.2 %copy-start.65 = (f32[128]{0:T(128)S(1)}, f32[128]{0:T(128)}, u32[]{:S(2)}) copy-start(f32[128]{0:T(128)} %copy-done.64) | copy-start | bytes 1540
  878.9 65.3 %all-to-all-start.2 = ((bf16[32,48,1536]{2,1,0:T(8,128)(2,1)}), bf16[32,48,1536]{2,1,0:T(8,128)(2,1)}, u32[]{:S(2)}, u32[]{:S(2)}) async-start(bf16[32,48,1536]{2,1,0:T(8,128)(2,1)} %convolution_convert_fusion.4), calls=%async_computation.2 | async-start | bytes 9437184 | tf_op jit(solution)/shard_map/all_to_all | solution.py:235
  884.4 223.6 %all-gather.14.cloned.1.call-start = ((), (), s32[]{:S(2)}) async-start(), calls=%async_computation.13 | async-start | bytes 1585152 | tf_op jit(solution)/shard_map/all_gather | solution.py:76
  884.7 8.5 copy-start.7
  955.9 8.5 copy-start.9
  964.4 14.7 %copy-start.74 = (f32[128]{0:T(128)S(1)}, f32[128]{0:T(128)}, u32[]{:S(2)}) copy-start(f32[128]{0:T(128)} %get-tuple-element.51) | copy-start | bytes 1540
  968.3 80.0 %copy-start.5 = (f32[128,1536]{1,0:T(8,128)S(1)}, f32[128,1536]{1,0:T(8,128)}, u32[]{:S(2)}) copy-start(f32[128,1536]{1,0:T(8,128)} %copy-done.4) | copy-start | bytes 2359300
  1043.6 67.0 %all-to-all-start.5 = ((bf16[4,12,7168]{2,1,0:T(8,128)(2,1)}), bf16[4,12,7168]{2,1,0:T(8,128)(2,1)S(1)}, u32[]{:S(2)}, u32[]{:S(2)}) async-start(bf16[4,12,7168]{2,1,0:T(8,128)(2,1)} %reshape.429), calls=%async_computation.6 | async-start | bytes 1835008 | tf_op jit(solution)/shard_map/all_to_all | solution.py:71
  1185.5 8.1 copy-start.13
  1185.5 8.1 copy-start.25
  (58 other events, 291.1 us)
Sparse Core Ops, SparseCore 0:
  12.5 102.4 all-gather.11
  151.4 52.1 all-gather.7
  764.3 88.8 reduce-scatter.9
  855.6 50.7 reduce-scatter.11
  910.7 130.6 reduce-scatter.7
  1044.6 63.4 all-gather.13
Sparse Core Ops, SparseCore 1:
  359.5 54.1 all-gather.9
where the time goes:
time: 1220 us; the launch traced here: 1210 us
  waiting for transfers between devices  426 us (35%)
  local copies, waits for them, and re-layouts  410 us (34%)
  matrix products  159 us (13%)
  other arithmetic  91.5 us (8%)
  blocking collectives  62.7 us (5%)
  starting transfers between devices  36.4 us (3%)
  between operations  20.9 us (2%)
    scatter x1, local copies, waits for them, and re-layouts, shards(): grad_outgoing = jnp.zeros((expert_count, capacity, model_width), jnp.bflo...  120 us
    scatter x1, local copies, waits for them, and re-layouts, shards(): outgoing = jnp.zeros((expert_count, capacity, model_width), jnp.bfloat16)...  120 us
    unnamed x206, local copies, waits for them, and re-layouts  109 us
    all_gather x1, waiting for transfers between devices, shards(): lax.all_gather(dense_low, ('ctx', 'wt', 'seq'), axis=0, tiled=True)  103 us
    unnamed x1, blocking collectives  62.7 us
    reduce_scatter x1, waiting for transfers between devices, shards(): lax.psum_scatter(jnp.concatenate([product(h_one, grad_qkv), product(grad_...  62.3 us
    all_gather x1, waiting for transfers between devices, gathered_total(): return lax.all_gather(array, axis).sum(0)  57.5 us
    all_to_all x1, waiting for transfers between devices, shards(): lax.all_to_all(grad_rows.reshape(expert_count, capacity, model_width).ast...  52.1 us
  transfers between devices with their start and end apart: 13, of which 9 were waited for; matrix products, arithmetic and copies ran while one was open for 26% of the time, Pallas kernels for 0%

commit v1 on v0

v1 whole, which is shorter than its diff:
```python
import functools

import jax
import jax.numpy as jnp
from jax import lax
from jax.experimental import pallas as pl
from jax.experimental.layout import Layout, with_layout_constraint
from jax.experimental.pallas import tpu as pltpu
from jax.sharding import Mesh
from jax.sharding import PartitionSpec as P

HEADS = 12
KV_HEADS = 4
HEAD_DIM = 128
GROUP = HEADS // KV_HEADS
EXPERT_FF = 512
SHARED_FF = 1024
TOP = 6
STEP = 10

EPS_NORM = 1e-05
CLIP_NORM = 1.0
FIRST_DECAY = 0.9
SECOND_DECAY = 0.95
ADAM_EPS = 1e-08
WEIGHT_DECAY = 0.1
MATRIX_RATE = 0.05
GAIN_RATE = 0.6
NEGATIVE = -1e30

QW = HEADS * HEAD_DIM
KW = KV_HEADS * HEAD_DIM
STARTS = (0, QW, QW + KW, QW + 2 * KW, 2 * QW + 2 * KW, 2 * QW + 2 * KW + SHARED_FF, 2 * QW + 2 * KW + 2 * SHARED_FF)
WIDTHS = (QW, KW, KW, QW, SHARED_FF, SHARED_FF, SHARED_FF)
HALF_WIDTHS = tuple(w // 2 for w in WIDTHS)
HALF_COLS = sum(HALF_WIDTHS)
QKV_HALF = sum(HALF_WIDTHS[:3])
HEADS_HALF = HEADS // 2
KV_HALF = KV_HEADS // 2

CHIPS = ("y", "x")
CTX = ("y", "x", "core")
DEPTH = ("wt", "seq")
COLUMN = ("core", "wt", "seq")
ALL = CTX + DEPTH
BF = jnp.bfloat16
F32 = jnp.float32
LOG2E = 1.4426950408889634
VMEM_LIMIT = 48 << 20


def turn(v, phase, step):
    pairs = []
    for y in range(4):
        for x in range(4):
            for core in range(2):
                along_x = (phase == 1) == (core == 0)
                ty, tx = (y, (x + step) % 4) if along_x else ((y + step) % 4, x)
                pairs.append(((y * 4 + x) * 2 + core, (ty * 4 + tx) * 2 + core))
    return lax.ppermute(v, CTX, pairs)


def swap(v):
    return lax.ppermute(v, "core", [(0, 1), (1, 0)])


def middle(rows):
    return (rows // 2 + 7) // 8 * 8


def ring_gather(v, phase):
    left = turn(v, phase, 1)
    right = turn(v, phase, -1)
    half = middle(v.shape[0])
    far_a = turn(left[:half], phase, 1)
    far_b = turn(right[half:], phase, -1)
    return jnp.concatenate([v, left, right, far_a, far_b], axis=0)


def gather_plane(v):
    return ring_gather(ring_gather(v, 1), 2)


def ring_sum(g, phase):
    rows = g.shape[0] // 4
    own, left, right, far = (g[k * rows : (k + 1) * rows] for k in range(4))
    half = middle(rows)
    from_left = turn(far[:half], phase, 1)
    from_right = turn(far[half:], phase, -1)
    to_right = jnp.concatenate(
        [(right[:half].astype(F32) + from_left.astype(F32)).astype(BF), right[half:]], axis=0
    )
    to_left = jnp.concatenate(
        [left[:half], (left[half:].astype(F32) + from_right.astype(F32)).astype(BF)], axis=0
    )
    one = turn(to_right, phase, 1)
    two = turn(to_left, phase, -1)
    return own.astype(F32) + one.astype(F32) + two.astype(F32)


def sum_plane(g):
    return ring_sum(ring_sum(g, 2).astype(BF), 1)


def block_chips(iy, ix, first_core):
    offsets = jnp.array([0, 3, 1, 2], jnp.int32)
    outer, inner = jnp.repeat(offsets, 4), jnp.tile(offsets, 4)
    y = (iy + jnp.where(first_core, outer, inner)) % 4
    x = (ix + jnp.where(first_core, inner, outer)) % 4
    return y * 4 + x


def row_major(v):
    return with_layout_constraint(v, Layout(tuple(range(v.ndim))))


def attend_kernel(scale, kpos_ref, qpos_ref, q_ref, kv_ref, out_ref, lse_ref, acc, top, total):
    step = pl.program_id(0)

    @pl.when(step == 0)
    def _():
        acc[...] = jnp.zeros_like(acc)
        total[...] = jnp.zeros_like(total)
        top[...] = jnp.full_like(top, -jnp.inf)

    spots = kpos_ref[...]
    visible = (spots >= qpos_ref[0:1, :]) & (spots <= qpos_ref[1:2, :])
    for head in range(HEADS_HALF):
        kv_head = head // GROUP
        cols = slice(head * HEAD_DIM, (head + 1) * HEAD_DIM)
        key = kv_ref[:, kv_head * HEAD_DIM : (kv_head + 1) * HEAD_DIM]
        value = kv_ref[:, (KV_HALF + kv_head) * HEAD_DIM : (KV_HALF + kv_head + 1) * HEAD_DIM]
        scores = times_transposed(key, q_ref[:, cols]) * (scale * LOG2E)
        scores = jnp.where(visible, scores, NEGATIVE)
        before = top[head : head + 1, :]
        now = jnp.maximum(before, jnp.max(scores, axis=0, keepdims=True))
        expo = jnp.exp2(scores - now)
        fade = jnp.exp2(before - now)
        top[head : head + 1, :] = now
        total[head : head + 1, :] = total[head : head + 1, :] * fade + jnp.sum(
            expo, axis=0, keepdims=True
        )
        acc[cols, :] = acc[cols, :] * fade + transposed_times(value, expo.astype(BF))

    @pl.when(step == pl.num_programs(0) - 1)
    def _():
        for head in range(HEADS_HALF):
            cols = slice(head * HEAD_DIM, (head + 1) * HEAD_DIM)
            out_ref[:, cols] = (acc[cols, :] / total[head : head + 1, :]).T
        lse_ref[...] = top[...] + jnp.log2(total[...])


def attend(key_spots, query_range, query, kv_all, scale):
    rows, cols = query.shape
    keys = kv_all.shape[0]
    block = 512
    return pl.pallas_call(
        functools.partial(attend_kernel, scale),
        grid=(keys // block,),
        in_specs=[
            pl.BlockSpec((block, 1), lambda j: (j, 0)),
            pl.BlockSpec((8, rows), lambda j: (0, 0)),
            pl.BlockSpec((rows, cols), lambda j: (0, 0)),
            pl.BlockSpec((block, kv_all.shape[1]), lambda j: (j, 0)),
        ],
        out_specs=[
            pl.BlockSpec((rows, cols), lambda j: (0, 0)),
            pl.BlockSpec((8, rows), lambda j: (0, 0)),
        ],
        out_shape=[
            jax.ShapeDtypeStruct((rows, cols), F32),
            jax.ShapeDtypeStruct((8, rows), F32),
        ],
        scratch_shapes=[
            pltpu.VMEM((cols, rows), F32),
            pltpu.VMEM((8, rows), F32),
            pltpu.VMEM((8, rows), F32),
        ],
        cost_estimate=pl.CostEstimate(
            flops=4 * rows * cols * keys, bytes_accessed=8 << 20, transcendentals=rows * keys * 6
        ),
        compiler_params=pltpu.CompilerParams(vmem_limit_bytes=VMEM_LIMIT),
    )(key_spots, query_range, query, kv_all)


def attend_back_kernel(
    scale, kpos_ref, qpos_ref, q_ref, do_ref, lse_ref, delta_ref, kv_ref, dq_ref, dkv_ref, acc
):
    step = pl.program_id(0)

    @pl.when(step == 0)
    def _():
        acc[...] = jnp.zeros_like(acc)

    spots = kpos_ref[...]
    visible = (spots >= qpos_ref[0:1, :]) & (spots <= qpos_ref[1:2, :])
    for kv_head in range(KV_HALF):
        k_cols = slice(kv_head * HEAD_DIM, (kv_head + 1) * HEAD_DIM)
        v_cols = slice((KV_HALF + kv_head) * HEAD_DIM, (KV_HALF + kv_head + 1) * HEAD_DIM)
        key, value = kv_ref[:, k_cols], kv_ref[:, v_cols]
        key_grad = jnp.zeros(key.shape, F32)
        value_grad = jnp.zeros(key.shape, F32)
        for member in range(GROUP):
            head = kv_head * GROUP + member
            cols = slice(head * HEAD_DIM, (head + 1) * HEAD_DIM)
            query, upstream = q_ref[:, cols], do_ref[:, cols]
            scores = times_transposed(key, query) * (scale * LOG2E)
            scores = jnp.where(visible, scores, NEGATIVE)
            chances = jnp.exp2(scores - lse_ref[head : head + 1, :])
            inner = times_transposed(value, upstream)
            grad_scores = (chances * (inner - delta_ref[head : head + 1, :])).astype(BF)
            value_grad += dot(chances.astype(BF), upstream)
            key_grad += dot(grad_scores, query)
            acc[cols, :] += transposed_times(key, grad_scores)
        dkv_ref[:, k_cols] = (key_grad * scale).astype(BF)
        dkv_ref[:, v_cols] = value_grad.astype(BF)

    @pl.when(step == pl.num_programs(0) - 1)
    def _():
        for head in range(HEADS_HALF):
            cols = slice(head * HEAD_DIM, (head + 1) * HEAD_DIM)
            dq_ref[:, cols] = (acc[cols, :] * scale).T.astype(BF)


def attend_back(key_spots, query_range, query, upstream, lse, delta, kv_all, scale):
    rows, cols = query.shape
    keys, kv_cols = kv_all.shape
    block = 512
    whole = pl.BlockSpec((rows, cols), lambda j: (0, 0))
    stats = pl.BlockSpec((8, rows), lambda j: (0, 0))
    some = pl.BlockSpec((block, kv_cols), lambda j: (j, 0))
    return pl.pallas_call(
        functools.partial(attend_back_kernel, scale),
        grid=(keys // block,),
        in_specs=[
            pl.BlockSpec((block, 1), lambda j: (j, 0)),
            stats,
            whole,
            whole,
            stats,
            stats,
            some,
        ],
        out_specs=[whole, some],
        out_shape=[
            jax.ShapeDtypeStruct((rows, cols), BF),
            jax.ShapeDtypeStruct((keys, kv_cols), BF),
        ],
        scratch_shapes=[pltpu.VMEM((cols, rows), F32)],
        cost_estimate=pl.CostEstimate(
            flops=10 * rows * cols * keys, bytes_accessed=12 << 20, transcendentals=rows * keys * 6
        ),
        compiler_params=pltpu.CompilerParams(vmem_limit_bytes=VMEM_LIMIT),
    )(key_spots, query_range, query, upstream, lse, delta, kv_all)


def pick_kernel(chips_ref, pick_ref, scale_ref, source_ref, out_ref):
    rows = dot(pick_ref[0], source_ref[0]) * scale_ref[0]
    cap = out_ref.shape[2]
    out_ref[0, 0] = rows[:cap].astype(BF)
    out_ref[1, 0] = rows[cap:].astype(BF)


def pick_rows(chips, pick, scale, source):
    blocks, slots, rows = pick.shape
    width = source.shape[2]
    return pl.pallas_call(
        pick_kernel,
        grid_spec=pltpu.PrefetchScalarGridSpec(
            num_scalar_prefetch=1,
            grid=(blocks,),
            in_specs=[
                pl.BlockSpec((1, slots, rows), lambda b, t: (b, 0, 0)),
                pl.BlockSpec((1, slots, 1), lambda b, t: (b, 0, 0)),
                pl.BlockSpec((1, rows, width), lambda b, t: (t[b], 0, 0)),
            ],
            out_specs=pl.BlockSpec((2, 1, slots // 2, width), lambda b, t: (0, b, 0, 0)),
        ),
        out_shape=jax.ShapeDtypeStruct((2, blocks, slots // 2, width), BF),
        cost_estimate=pl.CostEstimate(
            flops=2 * blocks * slots * rows * width, bytes_accessed=12 << 20, transcendentals=0
        ),
        compiler_params=pltpu.CompilerParams(vmem_limit_bytes=VMEM_LIMIT),
    )(chips, pick, scale, source)


def unpick_kernel(pick_ref, scale_ref, rows_ref, out_ref):
    rows = jnp.concatenate([rows_ref[0, 0], rows_ref[1, 0]], axis=0)
    rows = (rows.astype(F32) * scale_ref[0]).astype(BF)
    out_ref[...] = transposed_times(pick_ref[0], rows).astype(BF)


def unpick_rows(pick, scale, given):
    blocks, slots, rows = pick.shape
    width = given.shape[3]
    return pl.pallas_call(
        unpick_kernel,
        grid=(blocks,),
        in_specs=[
            pl.BlockSpec((1, slots, rows), lambda b: (b, 0, 0)),
            pl.BlockSpec((1, slots, 1), lambda b: (b, 0, 0)),
            pl.BlockSpec((2, 1, slots // 2, width), lambda b: (0, b, 0, 0)),
        ],
        out_specs=pl.BlockSpec((rows, width), lambda b: (b, 0)),
        out_shape=jax.ShapeDtypeStruct((blocks * rows, width), BF),
        cost_estimate=pl.CostEstimate(
            flops=2 * blocks * slots * rows * width, bytes_accessed=12 << 20, transcendentals=0
        ),
        compiler_params=pltpu.CompilerParams(vmem_limit_bytes=VMEM_LIMIT),
    )(pick, scale, given)


def total_over_all(v):
    v = v + swap(v)
    for axis in ("x", "y"):
        v = v + lax.ppermute(v, axis, [(i, i ^ 1) for i in range(4)])
        v = v + lax.ppermute(v, axis, [(i, i ^ 3) for i in range(4)])
    for axis in DEPTH:
        v = v + lax.ppermute(v, axis, [(0, 1), (1, 0)])
    return v


def silu_parts(values):
    sigmoid_values = jax.nn.sigmoid(values)
    return (values * sigmoid_values, sigmoid_values * (1.0 + values * (1.0 - sigmoid_values)))


def norm_forward(values, gain_row):
    factor = lax.rsqrt(jnp.mean(values * values, axis=-1, keepdims=True) + EPS_NORM)
    normed = values * factor
    return (normed * gain_row, normed, factor)


def norm_backward(upstream, normed, factor, gain_row):
    scaled = upstream * gain_row
    inward = factor * (scaled - normed * jnp.mean(scaled * normed, axis=-1, keepdims=True))
    return (inward, jnp.sum(upstream * normed, axis=0))


def adamw_step(weight, first_moment, second, gradient, step_rate, decay_rate):
    first_moment = FIRST_DECAY * first_moment + (1.0 - FIRST_DECAY) * gradient
    second = SECOND_DECAY * second + (1.0 - SECOND_DECAY) * gradient * gradient
    first_hat = first_moment / (1.0 - FIRST_DECAY**STEP)
    second_hat = second / (1.0 - SECOND_DECAY**STEP)
    weight = weight - step_rate * (
        first_hat / (jnp.sqrt(second_hat) + ADAM_EPS) + decay_rate * weight
    )
    return (weight, first_moment, second)


def dot(left, right):
    return jnp.dot(left, right, preferred_element_type=F32)


def times_transposed(left, right):
    return lax.dot_general(left, right, (((1,), (1,)), ((), ())), preferred_element_type=F32)


def transposed_times(left, right):
    return lax.dot_general(left, right, (((0,), (0,)), ((), ())), preferred_element_type=F32)


def halves_of(dense):
    parts = []
    for core in range(2):
        parts.append(
            jnp.concatenate(
                [
                    dense[:, s + core * w : s + (core + 1) * w]
                    for s, w in zip(STARTS, HALF_WIDTHS, strict=True)
                ],
                axis=1,
            )
        )
    return parts


def whole_of(half0, half1):
    columns, at = [], 0
    for w in HALF_WIDTHS:
        columns += [half0[:, at : at + w], half1[:, at : at + w]]
        at += w
    return jnp.concatenate(columns, axis=1)


def shards(
    tokens,
    cotangent,
    segment_ids,
    routes,
    gates,
    dense_weights,
    dense_first,
    dense_second,
    expert_weights,
    expert_first,
    expert_second,
    gains,
    gain_first,
    gain_second,
):
    rows = tokens.shape[1]
    width = tokens.shape[2]
    seq_len = rows * 32
    cap = min(rows, 2 * rows * TOP // 32)
    scale = HEAD_DIM ** (-0.5)
    iy, ix, core = lax.axis_index("y"), lax.axis_index("x"), lax.axis_index("core")
    chip = iy * 4 + ix
    first_core = core == 0
    first_of_chip = chip * 2 * rows

    def both_cores(mine, other):
        return jnp.where(
            first_core,
            jnp.concatenate([mine, other], axis=0),
            jnp.concatenate([other, mine], axis=0),
        )

    def of_chip(v):
        return both_cores(v, swap(v))

    def own_rows(v):
        return lax.dynamic_slice_in_dim(v, core * rows, rows, 0)

    def other_rows(v):
        return lax.dynamic_slice_in_dim(v, (1 - core) * rows, rows, 0)

    def summed_for_own(v):
        return own_rows(v) + swap(other_rows(v))

    def three_terms(v):
        high = v.astype(BF)
        rest = v - high.astype(F32)
        mid = rest.astype(BF)
        return [high, mid, (rest - mid.astype(F32)).astype(BF)]

    segments_chip = of_chip(segment_ids[0][None].astype(F32)).reshape(1, 2 * rows)
    digits = jnp.concatenate(
        [jnp.floor(segments_chip / 64.0), segments_chip - 64.0 * jnp.floor(segments_chip / 64.0)],
        axis=0,
    ).astype(BF)
    small = jnp.concatenate(
        [digits.reshape(4, rows), routes[0].T.astype(BF), *three_terms(gates[0].T)], axis=0
    )
    small_rows = small.shape[0]
    small = jnp.pad(small.reshape(-1), (0, 8 * QKV_HALF - small.size)).reshape(8, QKV_HALF)

    dense_low = dense_weights.astype(BF)
    dense_both = jnp.stack(halves_of(dense_low))[:, None]
    dense_both = jnp.broadcast_to(dense_both, (2, 4, *dense_low.shape[:1], HALF_COLS))
    chip_rows = 8 * dense_low.shape[0]
    dense_half = lax.all_to_all(
        dense_both.reshape(8, -1, HALF_COLS), COLUMN, 0, 0, tiled=True
    ).reshape(chip_rows, HALF_COLS)
    chips = block_chips(iy, ix, first_core)
    qkv_all = gather_plane(jnp.concatenate([dense_half[:, :QKV_HALF], small], axis=0))
    qkv_all = qkv_all.reshape(16, chip_rows + 8, QKV_HALF)
    w_qkv = qkv_all[:, :chip_rows].reshape(16 * chip_rows, QKV_HALF)
    small_all = qkv_all[:, chip_rows:].reshape(16, -1)[:, : small_rows * rows]
    small_all = small_all.reshape(16, small_rows, rows).astype(F32)
    w_rest = lax.all_gather(dense_half[:, QKV_HALF:], CHIPS, axis=0, tiled=True)
    w_o = w_rest[:, : HALF_WIDTHS[3]]
    at = HALF_WIDTHS[3]
    w_gu = w_rest[:, at : at + 2 * HALF_WIDTHS[4]]
    w_d = w_rest[:, at + 2 * HALF_WIDTHS[4] :]

    expert_own = lax.all_gather(expert_weights[0].astype(BF), DEPTH, axis=0, tiled=True)
    expert_other = swap(expert_own)
    experts = [
        jnp.where(first_core, expert_own, expert_other),
        jnp.where(first_core, expert_other, expert_own),
    ]

    places = jnp.arange(width, dtype=jnp.int32)
    source = jnp.repeat(chips, chip_rows) * chip_rows + places % chip_rows
    order = (places[:, None] == source[None, :]).astype(BF)

    inputs = tokens[0].astype(F32)
    h_one_f, normed_one, factor_one = norm_forward(inputs, gains[0])
    h_one = dot(of_chip(h_one_f.astype(BF)), order).astype(BF)
    upstream = cotangent[0]
    upstream_f = upstream.astype(F32)
    cot_all = lax.all_gather(upstream, CHIPS, axis=0, tiled=True).reshape(16, rows, width)
    cot_chip = of_chip(upstream)

    projected = dot(h_one, w_qkv)
    query = projected[:, : HALF_WIDTHS[0]].astype(BF)
    kv_all = gather_plane(projected[:, HALF_WIDTHS[0] :].astype(BF))

    segments_all = (small_all[:, :2] * 64.0 + small_all[:, 2:4]).reshape(-1)
    routes_all = small_all[:, 4 : 4 + TOP]
    high, mid_term, low_term = (
        small_all[:, 4 + k * TOP : 4 + (k + 1) * TOP] for k in range(1, 4)
    )
    gates_all = high + mid_term + low_term
    earlier = jnp.triu(jnp.ones((rows, rows), F32), 1).astype(BF)
    picks, gate_slots = [], []
    for local in range(2):
        named = routes_all == (chip * 2 + local).astype(F32)
        hit = jnp.any(named, axis=1)
        gate = jnp.sum(jnp.where(named, gates_all, 0.0), axis=1)
        slot = dot(hit.astype(BF), earlier).astype(jnp.int32)
        pick = hit[:, None, :] & (
            slot[:, None, :] == jnp.arange(cap, dtype=jnp.int32)[None, :, None]
        )
        picks.append(pick.astype(BF))
        gate_slots.append(jnp.sum(jnp.where(pick, gate[:, None, :], 0.0), axis=2, keepdims=True))
    pick = jnp.concatenate(picks, axis=1)
    gate_slot = jnp.concatenate(gate_slots, axis=1)
    ones = jnp.ones_like(gate_slot)

    query_spots = first_of_chip + jnp.arange(2 * rows, dtype=jnp.int32)
    run_start = jnp.sum(
        (segments_all[None, :] < segments_chip.reshape(-1, 1)).astype(jnp.int32), axis=1
    )
    query_range = jnp.concatenate(
        [run_start[None], query_spots[None], jnp.zeros((6, 2 * rows), jnp.int32)], axis=0
    )
    key_spots = (
        chips[:, None] * (2 * rows) + jnp.arange(2 * rows, dtype=jnp.int32)[None, :]
    ).reshape(-1, 1)
    attn_f, lse = attend(key_spots, query_range, query, kv_all, scale)
    attn = attn_f.astype(BF)
    resid = inputs + summed_for_own(times_transposed(attn, w_o))
    h_two_f, normed_two, factor_two = norm_forward(resid, gains[1])
    h_two = h_two_f.astype(BF)

    h_two_all = gather_plane(h_two).reshape(16, rows, width)
    h_two_chip = of_chip(h_two)
    x_both = pick_rows(jnp.arange(16, dtype=jnp.int32), pick, ones, h_two_all)
    d_out_both = pick_rows(chips, pick, gate_slot, cot_all)
    outs, d_xs, expert_grads = [], [], []
    for local in range(2):
        weights = experts[local]
        x = x_both[local].reshape(16 * cap, width)
        pre = dot(x, weights[:, : 2 * EXPERT_FF])
        gate_pre, up_pre = pre[:, :EXPERT_FF], pre[:, EXPERT_FF:]
        act, deriv = silu_parts(gate_pre)
        mid = (act * up_pre).astype(BF)
        outs.append(times_transposed(mid, weights[:, 2 * EXPERT_FF :]).astype(BF))
        d_out = d_out_both[local].reshape(16 * cap, width)
        d_mid = dot(d_out, weights[:, 2 * EXPERT_FF :])
        d_pre = jnp.concatenate(
            [(d_mid * up_pre * deriv).astype(BF), (d_mid * act).astype(BF)], axis=1
        )
        d_xs.append(times_transposed(d_pre, weights[:, : 2 * EXPERT_FF]).astype(BF))
        expert_grads.append(
            jnp.concatenate(
                [
                    row_major(transposed_times(x, d_pre).astype(BF)),
                    row_major(transposed_times(d_out, mid).astype(BF)),
                ],
                axis=1,
            )
        )
    d_x_both = jnp.stack(d_xs).reshape(2, 16, cap, width)
    grad_h_experts = sum_plane(unpick_rows(pick, ones, d_x_both))
    out_both = jnp.stack(outs).reshape(2, 16, cap, width)
    mixture = sum_plane(unpick_rows(pick, gate_slot, out_both))

    own_part = jnp.where(first_core, expert_grads[0], expert_grads[1])
    other_part = jnp.where(first_core, expert_grads[1], expert_grads[0])
    expert_local = row_major((own_part.astype(F32) + swap(other_part).astype(F32)).astype(BF))
    expert_grad = lax.psum_scatter(expert_local, DEPTH, scatter_dimension=0, tiled=True)
    expert_grad = row_major(expert_grad).astype(F32)

    shared_pre = dot(h_two_chip, w_gu)
    half_ff = HALF_WIDTHS[4]
    shared_gate, shared_up = shared_pre[:, :half_ff], shared_pre[:, half_ff:]
    shared_act, shared_deriv = silu_parts(shared_gate)
    shared_mid = (shared_act * shared_up).astype(BF)
    shared_out = summed_for_own(times_transposed(shared_mid, w_d))
    block_out = (resid + shared_out + mixture).astype(BF)
    grad_shared_mid = dot(cot_chip, w_d)
    grad_shared = jnp.concatenate(
        [
            (grad_shared_mid * shared_up * shared_deriv).astype(BF),
            (grad_shared_mid * shared_act).astype(BF),
        ],
        axis=1,
    )
    grad_h_two = summed_for_own(times_transposed(grad_shared, w_gu)) + grad_h_experts
    grad_resid_norm, gain_two_part = norm_backward(grad_h_two, normed_two, factor_two, gains[1])
    grad_resid = upstream_f + grad_resid_norm
    grad_att = of_chip(grad_resid.astype(BF))
    grad_attn = dot(grad_att, w_o).astype(BF)

    delta = jnp.sum(
        (grad_attn.astype(F32) * attn_f).reshape(2 * rows, HEADS_HALF, HEAD_DIM), axis=2
    ).T
    delta = jnp.pad(delta, ((0, 8 - HEADS_HALF), (0, 0)))
    grad_query, kv_terms = attend_back(
        key_spots, query_range, query, grad_attn, lse, delta, kv_all, scale
    )
    grad_kv = sum_plane(kv_terms).astype(BF)
    grad_qkv = jnp.concatenate([grad_query, grad_kv], axis=1)
    grad_h_one = times_transposed(grad_qkv, w_qkv).astype(BF)
    grad_h_one = summed_for_own(times_transposed(grad_h_one, order).astype(BF).astype(F32))
    grad_input_norm, gain_one_part = norm_backward(grad_h_one, normed_one, factor_one, gains[0])
    input_grad = grad_resid + grad_input_norm

    grads_rest = jnp.concatenate(
        [
            row_major(transposed_times(grad_att, attn).astype(BF)),
            row_major(transposed_times(h_two_chip, grad_shared).astype(BF)),
            row_major(transposed_times(cot_chip, shared_mid).astype(BF)),
        ],
        axis=1,
    )
    rest_sum = lax.psum_scatter(grads_rest, CHIPS, scatter_dimension=0, tiled=True)
    qkv_sum = sum_plane(transposed_times(h_one, grad_qkv).astype(BF))
    half_sum = jnp.concatenate([qkv_sum.astype(BF), rest_sum], axis=1)
    blocks = lax.all_to_all(
        half_sum.reshape(8, chip_rows // 8, HALF_COLS), COLUMN, 0, 0, tiled=True
    )
    blocks = jnp.sum(blocks.reshape(2, 4, chip_rows // 8, HALF_COLS).astype(F32), axis=1)
    dense_grad = whole_of(blocks[0], blocks[1])

    gain_part = jnp.stack([gain_one_part, gain_two_part])
    local_squares = jnp.sum(dense_grad * dense_grad) + jnp.sum(expert_grad * expert_grad)
    gain_tiles = gain_part.size // 128
    packed = jnp.concatenate(
        [
            gain_part.reshape(gain_tiles, 128),
            jnp.broadcast_to(local_squares, (8, 128)),
        ],
        axis=0,
    )
    packed = total_over_all(packed)
    gain_grad = packed[:gain_tiles].reshape(gain_part.shape)
    total_squares = packed[gain_tiles, 0]
    grad_norm = jnp.sqrt(total_squares + jnp.sum(gain_grad * gain_grad))
    clip_factor = jnp.minimum(1.0, CLIP_NORM / (grad_norm + 1e-06))
    dense_new, dense_first_new, dense_second_new = adamw_step(
        dense_weights,
        dense_first,
        dense_second,
        dense_grad * clip_factor,
        MATRIX_RATE,
        WEIGHT_DECAY,
    )
    expert_new, expert_first_new, expert_second_new = adamw_step(
        expert_weights,
        expert_first,
        expert_second,
        expert_grad[None] * clip_factor,
        MATRIX_RATE,
        WEIGHT_DECAY,
    )
    gain_cols = gain_first.shape[1]
    gain_begin = lax.axis_index(ALL) * gain_cols
    gain_slice = lax.dynamic_slice_in_dim(gains, gain_begin, gain_cols, 1)
    gain_grad_slice = lax.dynamic_slice_in_dim(gain_grad, gain_begin, gain_cols, 1)
    gain_new, gain_first_new, gain_second_new = adamw_step(
        gain_slice, gain_first, gain_second, gain_grad_slice * clip_factor, GAIN_RATE, 0.0
    )
    return (
        block_out[None],
        input_grad[None],
        grad_norm,
        dense_new,
        dense_first_new,
        dense_second_new,
        expert_new,
        expert_first_new,
        expert_second_new,
        gain_new,
        gain_first_new,
        gain_second_new,
    )


def solution(mesh):
    fine = Mesh(mesh.devices.reshape(4, 4, 2, 2, 2), ALL)
    sequence = (DEPTH, CTX)
    token = P(*sequence, None)
    dense = P(ALL, None)
    expert = P(CTX, DEPTH, None)
    gain = P(None, ALL)
    return jax.shard_map(
        shards,
        mesh=fine,
        in_specs=(
            token,
            token,
            P(*sequence),
            token,
            token,
            dense,
            dense,
            dense,
            expert,
            expert,
            expert,
            P(),
            gain,
            gain,
        ),
        out_specs=(
            token,
            token,
            P(),
            dense,
            dense,
            dense,
            expert,
            expert,
            expert,
            gain,
            gain,
            gain,
        ),
        check_vma=False,
    )
```

time: 1220 us -> 642 us (0.53)
  local copies, waits for them, and re-layouts: 410 us -> 72.3 us
  waiting for transfers between devices: 426 us -> 190 us
  matrix products: 159 us -> 61.6 us
  Pallas kernels: 0 us -> 83.9 us
  starting transfers between devices: 36.4 us -> 107 us
  blocking collectives: 62.7 us -> 21.5 us
  other arithmetic: 91.5 us -> 74.7 us
    scatter x2 -> x0, local copies, waits for them, and re-layouts: 240 us -> none  [the longest x1 120 us: shards(): grad_outgoing = jnp.zeros((expert_count, capacity, model_width), jnp.bflo...]
    all_gather x4 -> x3, waiting for transfers between devices: 195 us -> 0.02 us  [the longest x1 0.02 us: shards(): w_rest = lax.all_gather(dense_half[:, QKV_HALF:], CHIPS, axis=0, tiled=True)]
    ppermute x0 -> x74, waiting for transfers between devices: none -> 182 us  [the longest x56 162 us: turn(): return lax.ppermute(v, CTX, pairs)]
    all_to_all x6 -> x1, waiting for transfers between devices: 150 us -> 8.01 us  [shards(): lax.all_to_all(half_sum.reshape(8, chip_rows // 8, HALF_COLS), COLUMN, 0,...]
    ppermute x0 -> x74, starting transfers between devices: none -> 102 us  [the longest x56 94.3 us: turn(): return lax.ppermute(v, CTX, pairs)]
    dot_general x34 -> x11, matrix products: 123 us -> 22.4 us  [dot(): return jnp.dot(left, right, preferred_element_type=F32)]
    pallas_call x0 -> x6, Pallas kernels: none -> 83.9 us  [the longest x2 22.4 us: pick_rows(): pl.pallas_call(pick_kernel, grid_spec=pltpu.PrefetchScalarGridSpec(num_sc...]
    unnamed x206 -> x223, local copies, waits for them, and re-layouts: 109 us -> 35 us
  transfers between devices with their start and end apart: 13 -> 80, of which waited for: 9 -> 38; matrix products, arithmetic and copies ran while one was open for 26% -> 25% of each run, Pallas kernels for 0% -> 10%
where the time goes in v1:
time: 642 us; the launch traced here: 631 us
  waiting for transfers between devices  190 us (30%)
  starting transfers between devices  107 us (17%)
  Pallas kernels  83.9 us (13%)
  other arithmetic  74.7 us (12%)
  local copies, waits for them, and re-layouts  72.3 us (11%)
  matrix products  61.6 us (10%)
  blocking collectives  21.5 us (3%)
  between operations  20.1 us (3%)
    ppermute x56, waiting for transfers between devices, turn(): return lax.ppermute(v, CTX, pairs)  162 us
    ppermute x56, starting transfers between devices, turn(): return lax.ppermute(v, CTX, pairs)  94.3 us
    unnamed x223, local copies, waits for them, and re-layouts  35 us
    dot_general x8, matrix products, times_transposed(): lax.dot_general(left, right, (((1,), (1,)), ((), ())), preferred_element_...  23.4 us
    pallas_call x2, Pallas kernels, pick_rows(): pl.pallas_call(pick_kernel, grid_spec=pltpu.PrefetchScalarGridSpec(num_sc...  22.4 us
    dot_general x11, matrix products, dot(): return jnp.dot(left, right, preferred_element_type=F32)  22.4 us
    pallas_call x1, Pallas kernels, attend(): pl.pallas_call(functools.partial(attend_kernel, scale), grid=(keys // blo...  21.9 us
    all_to_all x1, blocking collectives, shards(): lax.all_to_all(dense_both.reshape(8, -1, HALF_COLS), COLUMN, 0, 0, tiled=...  21.5 us
  transfers between devices with their start and end apart: 80, of which 38 were waited for; matrix products, arithmetic and copies ran while one was open for 25% of the time, Pallas kernels for 10%

profile of v1, /device:TPU:0, one launch (start us, length us, event | category | flops | bytes accessed | tf_op | source)
XLA Modules:
  0.0 630.8 jit_solution(4284108840468463011)
XLA Ops:
  10.5 21.5 %all_to_all.10 = bf16[8,12,3584]{2,1,0:T(8,128)(2,1)S(1)} all-to-all(bf16[8,12,3584]{2,1,0:T(8,128)(2,1)S(1)} %bitcast.126), channel_id=1, replica_groups=mesh['y'=4,'x'=4,'core'=2,'wt'=2,'seq'=2] {'core','wt','seq'}, dimensions={0} | all-to-all | bytes 1376256 | tf_op jit(solution)/shard_map/all_to_all | solution.py:452
  39.9 3.3 collective-permute-done.1
  54.8 3.6 fusion.15
  58.4 9.1 %collective-permute-done.5 = bf16[416,1280]{1,0:T(8,128)(2,1)S(1)} collective-permute-done((bf16[416,1280]{1,0:T(8,128)(2,1)}, bf16[416,1280]{1,0:T(8,128)(2,1)S(1)}, u32[]{:S(2)}, u32[]{:S(2)}) %collective-permute-start.5) | collective-permute-done | bytes 1064992 | tf_op jit(solution)/shard_map/ppermute | solution.py:60
  71.1 7.0 %collective-permute-done.7 = bf16[208,1280]{1,0:T(8,128)(2,1)S(1)} collective-permute-done((bf16[208,1280]{1,0:T(8,128)(2,1)S(1)}, bf16[208,1280]{1,0:T(8,128)(2,1)S(1)}, u32[]{:S(2)}, u32[]{:S(2)}) %collective-permute-start.7) | collective-permute-done | bytes 532512 | tf_op jit(solution)/shard_map/ppermute | solution.py:60
  83.1 3.2 collective-permute-start.11
  88.3 4.2 collective-permute-done.10
  92.7 3.8 collective-permute-start.13
  102.7 3.3 collective-permute-start.15
  107.8 32.2 %collective-permute-done.14 = bf16[1024,512]{1,0:T(8,128)(2,1)S(1)} collective-permute-done((bf16[1024,512]{1,0:T(8,128)(2,1)}, bf16[1024,512]{1,0:T(8,128)(2,1)S(1)}, u32[]{:S(2)}, u32[]{:S(2)}) %collective-permute-start.14) | collective-permute-done | bytes 1048608 | tf_op jit(solution)/shard_map/ppermute | solution.py:60
  143.3 3.3 collective-permute-start.17
  156.5 21.9 %shard_map.238 = (f32[256,768]{1,0:T(8,128)S(1)}, f32[8,256]{1,0:T(8,128)S(1)}) custom-call(s32[4096,1]{1,0:T(8,128)S(1)} %bitcast.112, s32[8,256]{1,0:T(8,128)S(1)} %add_add_fusion.1.qpos_ref, bf16[256,768]{1,0:T(8,128)(2,1)S(1)} %slice.632.q_ref, bf16[4096,512]{1,0:T(8,128)(2,1)} %constant_dynamic-update-slice_fusion.35.kv_ref), custom_call_target="tpu_custom_call" | custom-call | flops 3221225472 | bytes 8388608 | tf_op jit(solution)/shard_map/pallas_call | solution.py:157
  190.5 12.2 %collective-permute-done.21 = bf16[128,1536]{1,0:T(8,128)(2,1)} collective-permute-done((bf16[128,1536]{1,0:T(8,128)(2,1)}, bf16[128,1536]{1,0:T(8,128)(2,1)}, u32[]{:S(2)}, u32[]{:S(2)}) %collective-permute-start.21) | collective-permute-done | bytes 393248 | tf_op jit(solution)/shard_map/ppermute | solution.py:60
  204.7 3.3 collective-permute-start.24
  219.6 8.0 %broadcast_select_fusion.2 = (bf16[1536,1536]{1,0:T(8,128)(2,1)}, bf16[1536,1536]{1,0:T(8,128)(2,1)}) fusion(bf16[1536,1536]{1,0:T(8,128)(2,1)} %collective-permute-done.29, pred[]{:T(512)S(6)} %eq.59, bf16[1,1536,1536]{2,1,0:T(8,128)(2,1)} %all-gather.8.cloned.1.call-done), kind=kLoop, calls=%fused_computation.14 | loop fusion | flops 4718592 | bytes 18874368 | tf_op jit(solution)/shard_map/jit(_where)/select_n | solution.py:470
  227.5 11.0 %shard_map.241 = bf16[2,16,48,1536]{3,2,1,0:T(8,128)(2,1)S(1)} custom-call(s32[16]{0:T(128)S(1)} %get-tuple-element.44.chips_ref, bf16[16,96,128]{2,1,0:T(8,128)(2,1)S(1)} %add_convert_fusion.14.pick_ref, f32[16,96,1]{2,1,0:T(8,128)S(1)} %copy.54.scale_ref, bf16[16,128,1536]{2,1,0:T(8,128)(2,1)} %bitcast.114), custom_call_target="tpu_custom_call" | custom-call | flops 603979776 | bytes 12582912 | tf_op jit(solution)/shard_map/pallas_call | solution.py:267
  243.4 3.5 collective-permute-start.28
  257.4 11.4 %shard_map.239 = bf16[2,16,48,1536]{3,2,1,0:T(8,128)(2,1)S(1)} custom-call(s32[16]{0:T(128)S(1)} %iota.46.chips_ref, bf16[16,96,128]{2,1,0:T(8,128)(2,1)S(1)} %add_convert_fusion.14.pick_ref, f32[16,96,1]{2,1,0:T(8,128)S(1)} %broadcast_in_dim.95.scale_ref, bf16[16,128,1536]{2,1,0:T(8,128)(2,1)} %bitcast.17.source_ref), custom_call_target="tpu_custom_call" | custom-call | flops 603979776 | bytes 12582912 | tf_op jit(solution)/shard_map/pallas_call | solution.py:267
  287.2 9.4 %shard_map.242 = bf16[2048,1536]{1,0:T(8,128)(2,1)} custom-call(bf16[16,96,128]{2,1,0:T(8,128)(2,1)S(1)} %add_convert_fusion.14.pick_ref, f32[16,96,1]{2,1,0:T(8,128)S(1)} %broadcast_in_dim.95.scale_ref, bf16[2,16,48,1536]{3,2,1,0:T(8,128)(2,1)S(1)} %pad_maximum_fusion.2.rows_ref), custom_call_target="tpu_custom_call" | custom-call | flops 603979776 | bytes 12582912 | tf_op jit(solution)/shard_map/pallas_call | solution.py:296
  299.1 3.4 collective-permute-start.42
  302.6 9.9 %collective-permute-done.40 = bf16[256,1536]{1,0:T(8,128)(2,1)S(1)} collective-permute-done((bf16[256,1536]{1,0:T(8,128)(2,1)S(1)}, bf16[256,1536]{1,0:T(8,128)(2,1)S(1)}, u32[]{:S(2)}, u32[]{:S(2)}) %collective-permute-start.40) | collective-permute-done | bytes 786464 | tf_op jit(solution)/shard_map/ppermute | solution.py:60
  320.7 14.1 %collective-permute-done.41 = bf16[512,1536]{1,0:T(8,128)(2,1)S(1)} collective-permute-done((bf16[512,1536]{1,0:T(8,128)(2,1)S(1)}, bf16[512,1536]{1,0:T(8,128)(2,1)S(1)}, u32[]{:S(2)}, u32[]{:S(2)}) %collective-permute-start.41) | collective-permute-done | bytes 1572896 | tf_op jit(solution)/shard_map/ppermute | solution.py:60
  340.7 3.5 collective-permute-done.44
  344.4 3.3 collective-permute-start.47
  347.7 5.6 collective-permute-done.45
  359.6 3.4 pad_maximum_fusion
  363.4 3.4 convolution_convert_fusion.10
  375.6 3.3 broadcast_select_fusion
  385.4 9.4 %shard_map.240 = bf16[2048,1536]{1,0:T(8,128)(2,1)} custom-call(bf16[16,96,128]{2,1,0:T(8,128)(2,1)S(1)} %add_convert_fusion.14.pick_ref, f32[16,96,1]{2,1,0:T(8,128)S(1)} %copy.54.scale_ref, bf16[2,16,48,1536]{3,2,1,0:T(8,128)(2,1)S(1)} %pad_maximum_fusion.1.rows_ref), custom_call_target="tpu_custom_call" | custom-call | flops 603979776 | bytes 12582912 | tf_op jit(solution)/shard_map/pallas_call | solution.py:296
  394.8 3.7 fusion.110
  402.0 3.5 convert_multiply_fusion.4
  410.0 20.9 %shard_map.243 = (bf16[256,768]{1,0:T(8,128)(2,1)S(1)}, bf16[4096,512]{1,0:T(8,128)(2,1)}) custom-call(s32[4096,1]{1,0:T(8,128)S(1)} %bitcast.113, s32[8,256]{1,0:T(8,128)S(1)} %add_add_fusion.1.qpos_ref, bf16[256,768]{1,0:T(8,128)(2,1)S(1)} %copy-done.4, bf16[256,768]{1,0:T(8,128)(2,1)S(1)} %copy-done.5, f32[8,256]{1,0:T(8,128)S(1)} %get-tuple-element.17.lse_ref, ...), custom_call_target="tpu_custom_call" | custom-call | flops 8053063680 | bytes 12582912 | tf_op jit(solution)/shard_map/pallas_call | solution.py:232
  439.5 10.1 %collective-permute-done.49 = bf16[512,512]{1,0:T(8,128)(2,1)S(1)} collective-permute-done((bf16[512,512]{1,0:T(8,128)(2,1)S(1)}, bf16[512,512]{1,0:T(8,128)(2,1)S(1)}, u32[]{:S(2)}, u32[]{:S(2)}) %collective-permute-start.49) | collective-permute-done | bytes 524320 | tf_op jit(solution)/shard_map/ppermute | solution.py:60
  455.7 6.6 %add_convert_fusion = bf16[1536,1536]{1,0:T(8,128)(2,1)} fusion(bf16[1536,1536]{1,0:T(8,128)(2,1)} %collective-permute-done.66, pred[]{:T(512)S(6)} %eq.59, bf16[1536,512]{1,0:T(8,128)(2,1)S(1)} %copy-done.26, bf16[1536,1024]{1,0:T(8,128)(2,1)S(1)} %copy-done.13, bf16[1536,512]{1,0:T(8,128)(2,1)S(1)} %copy-done.24, bf16[1536,1024]{1,0:T(8,128)(2,1)S(1)} %copy-done.11), kind=kLoop, calls=%fused_computation | loop fusion | flops 30670848 | bytes 18874368 | tf_op jit(solution)/shard_map/convert_element_type | solution.py:563
  462.4 15.4 %collective-permute-done.50 = bf16[1024,512]{1,0:T(8,128)(2,1)} collective-permute-done((bf16[1024,512]{1,0:T(8,128)(2,1)S(1)}, bf16[1024,512]{1,0:T(8,128)(2,1)}, u32[]{:S(2)}, u32[]{:S(2)}) %collective-permute-start.50) | collective-permute-done | bytes 1048608 | tf_op jit(solution)/shard_map/ppermute | solution.py:60
  495.3 3.5 collective-permute-done.56
  512.3 3.3 collective-permute-start.61
  520.5 4.8 collective-permute-done.34
  533.8 6.2 fusion.17
  550.0 4.5 all-to-all-start.1
  560.6 8.0 %all-to-all-done.1 = bf16[8,12,3584]{2,1,0:T(8,128)(2,1)} async-done(((bf16[8,12,3584]{2,1,0:T(8,128)(2,1)}), bf16[8,12,3584]{2,1,0:T(8,128)(2,1)}, u32[]{:S(2)}, u32[]{:S(2)}) %all-to-all-start.1) | async-done | bytes 688160 | tf_op jit(solution)/shard_map/all_to_all | solution.py:613
  575.6 3.3 collective-permute-start.37
  579.7 4.3 collective-permute-done.68
  584.8 4.1 collective-permute-done.69
  589.2 3.7 collective-permute-done.70
  601.2 3.6 collective-permute-done.72
  605.7 3.4 fusion.51
  615.7 7.0 %multiply_subtract_fusion = (f32[1,384,1536]{2,1,0:T(8,128)}, f32[1,384,1536]{2,1,0:T(8,128)}, f32[1,384,1536]{2,1,0:T(8,128)}) fusion(f32[1,384,1536]{2,1,0:T(8,128)S(1)} %copy-done.17, f32[]{:T(128)S(6)} %min.3, bf16[384,1536]{1,0:T(8,128)(2,1)} %reduce-scatter.5.cloned.1.call-done, f32[1,384,1536]{2,1,0:T(8,128)} %param.24, f32[1,384,1536]{2,1,0:T(8,128)} %param.25), kind=kLoop, calls=%fused_computation.53 | loop fusion | flops 10027008 | bytes 15335428 | tf_op jit(solution)/shard_map/sub | solution.py:345
  (536 shorter events, 256.4 us)
Async XLA Ops:
  7.2 139.4 %all-gather.8.cloned.1.call-start = ((), (), s32[]{:S(2)}) async-start(), calls=%async_computation.7 | async-start | bytes 5898240 | tf_op jit(solution)/shard_map/all_gather | solution.py:467
  10.1 168.3 %all-gather.6.cloned.1.call-start = ((), (), s32[]{:S(2)}) async-start(), calls=%async_computation.4 | async-start | bytes 7520256 | tf_op jit(solution)/shard_map/all_gather | solution.py:461
  32.9 194.6 %all-gather.10.cloned.1.call-start = ((), (), s32[]{:S(2)}) async-start(), calls=%async_computation.8 | async-start | bytes 6684672 | tf_op jit(solution)/shard_map/all_gather | solution.py:483
  39.0 15.8 %collective-permute-start.9 = (bf16[128,1536]{1,0:T(8,128)(2,1)S(1)}, bf16[128,1536]{1,0:T(8,128)(2,1)}, u32[]{:S(2)}, u32[]{:S(2)}) collective-permute-start(bf16[128,1536]{1,0:T(8,128)(2,1)S(1)} %fusion.46), channel_id=1, source_target_pairs={{0,4},{4,0},{1,5},{5,1},{2,6},{6,2},{3,7},{7,3},{8,12},{12,8},{9,1... | collective-permute-start | bytes 1179656 | tf_op jit(solution)/shard_map/ppermute | solution.py:64
  39.3 508.5 %reduce-scatter.3.cloned.1.call-start = ((), (), s32[]{:S(2)}) async-start(), calls=%async_computation.5 | async-start | bytes 7520256 | tf_op jit(solution)/shard_map/reduce_scatter | solution.py:610
  51.0 16.4 %collective-permute-start.5 = (bf16[416,1280]{1,0:T(8,128)(2,1)}, bf16[416,1280]{1,0:T(8,128)(2,1)S(1)}, u32[]{:S(2)}, u32[]{:S(2)}) collective-permute-start(bf16[416,1280]{1,0:T(8,128)(2,1)} %get-tuple-element.156), channel_id=1, source_target_pairs={{0,32},{4,12},{8,40},{12,20},{16,48},{20,28},{24,56},{28,4},{32,64... | collective-permute-start | bytes 3194888 | tf_op jit(solution)/shard_map/ppermute | solution.py:60
  52.7 15.3 %collective-permute-start.6 = (bf16[416,1280]{1,0:T(8,128)(2,1)}, bf16[416,1280]{1,0:T(8,128)(2,1)S(1)}, u32[]{:S(2)}, u32[]{:S(2)}) collective-permute-start(bf16[416,1280]{1,0:T(8,128)(2,1)} %get-tuple-element.156), channel_id=1, source_target_pairs={{0,96},{4,28},{8,104},{12,4},{16,112},{20,12},{24,120},{28,20},{32... | collective-permute-start | bytes 3194888 | tf_op jit(solution)/shard_map/ppermute | solution.py:60
  67.5 10.5 %collective-permute-start.7 = (bf16[208,1280]{1,0:T(8,128)(2,1)S(1)}, bf16[208,1280]{1,0:T(8,128)(2,1)S(1)}, u32[]{:S(2)}, u32[]{:S(2)}) collective-permute-start(bf16[208,1280]{1,0:T(8,128)(2,1)S(1)} %slice.625), channel_id=1, source_target_pairs={{0,32},{4,12},{8,40},{12,20},{16,48},{20,28},{24,56},{28,4},{32,64... | collective-permute-start | bytes 1597448 | tf_op jit(solution)/shard_map/ppermute | solution.py:60
  68.0 10.1 %collective-permute-start.8 = (bf16[208,1280]{1,0:T(8,128)(2,1)S(1)}, bf16[208,1280]{1,0:T(8,128)(2,1)S(1)}, u32[]{:S(2)}, u32[]{:S(2)}) collective-permute-start(bf16[208,1280]{1,0:T(8,128)(2,1)S(1)} %slice.626), channel_id=1, source_target_pairs={{0,96},{4,28},{8,104},{12,4},{16,112},{20,12},{24,120},{28,20},{32... | collective-permute-start | bytes 1597448 | tf_op jit(solution)/shard_map/ppermute | solution.py:60
  83.1 9.4 %collective-permute-start.10 = (bf16[256,512]{1,0:T(8,128)(2,1)S(1)}, bf16[256,512]{1,0:T(8,128)(2,1)S(1)}, u32[]{:S(2)}, u32[]{:S(2)}) collective-permute-start(bf16[256,512]{1,0:T(8,128)(2,1)S(1)} %get-tuple-element.117), channel_id=1, source_target_pairs={{0,8},{4,36},{8,16},{12,44},{16,24},{20,52},{24,0},{28,60},{32,40}... | collective-permute-start | bytes 786440 | tf_op jit(solution)/shard_map/ppermute | solution.py:60
  83.1 9.6 %collective-permute-start.11 = (bf16[256,512]{1,0:T(8,128)(2,1)S(1)}, bf16[256,512]{1,0:T(8,128)(2,1)S(1)}, u32[]{:S(2)}, u32[]{:S(2)}) collective-permute-start(bf16[256,512]{1,0:T(8,128)(2,1)S(1)} %get-tuple-element.117), channel_id=1, source_target_pairs={{0,24},{4,100},{8,0},{12,108},{16,8},{20,116},{24,16},{28,124},{32... | collective-permute-start | bytes 786440 | tf_op jit(solution)/shard_map/ppermute | solution.py:60
  100.2 39.8 %collective-permute-start.14 = (bf16[1024,512]{1,0:T(8,128)(2,1)}, bf16[1024,512]{1,0:T(8,128)(2,1)S(1)}, u32[]{:S(2)}, u32[]{:S(2)}) collective-permute-start(bf16[1024,512]{1,0:T(8,128)(2,1)} %get-tuple-element.152), channel_id=1, source_target_pairs={{0,32},{4,12},{8,40},{12,20},{16,48},{20,28},{24,56},{28,4},{32,64... | collective-permute-start | bytes 3145736 | tf_op jit(solution)/shard_map/ppermute | solution.py:60
  102.7 38.8 %collective-permute-start.15 = (bf16[1024,512]{1,0:T(8,128)(2,1)}, bf16[1024,512]{1,0:T(8,128)(2,1)}, u32[]{:S(2)}, u32[]{:S(2)}) collective-permute-start(bf16[1024,512]{1,0:T(8,128)(2,1)} %get-tuple-element.152), channel_id=1, source_target_pairs={{0,96},{4,28},{8,104},{12,4},{16,112},{20,12},{24,120},{28,20},{32... | collective-permute-start | bytes 3145736 | tf_op jit(solution)/shard_map/ppermute | solution.py:60
  140.9 11.8 %collective-permute-start.16 = (bf16[512,512]{1,0:T(8,128)(2,1)}, bf16[512,512]{1,0:T(8,128)(2,1)}, u32[]{:S(2)}, u32[]{:S(2)}) collective-permute-start(bf16[512,512]{1,0:T(8,128)(2,1)} %slice.636), channel_id=1, source_target_pairs={{0,32},{4,12},{8,40},{12,20},{16,48},{20,28},{24,56},{28,4},{32,64... | collective-permute-start | bytes 1572872 | tf_op jit(solution)/shard_map/ppermute | solution.py:60
  143.3 11.2 %collective-permute-start.17 = (bf16[512,512]{1,0:T(8,128)(2,1)}, bf16[512,512]{1,0:T(8,128)(2,1)}, u32[]{:S(2)}, u32[]{:S(2)}) collective-permute-start(bf16[512,512]{1,0:T(8,128)(2,1)} %slice.637), channel_id=1, source_target_pairs={{0,96},{4,28},{8,104},{12,4},{16,112},{20,12},{24,120},{28,20},{32... | collective-permute-start | bytes 1572872 | tf_op jit(solution)/shard_map/ppermute | solution.py:60
  146.6 72.9 %collective-permute-start.29 = (bf16[1536,1536]{1,0:T(8,128)(2,1)}, bf16[1536,1536]{1,0:T(8,128)(2,1)}, u32[]{:S(2)}, u32[]{:S(2)}) collective-permute-start(bf16[1536,1536]{1,0:T(8,128)(2,1)} %bitcast.119), channel_id=1, source_target_pairs={{0,4},{4,0},{1,5},{5,1},{2,6},{6,2},{3,7},{7,3},{8,12},{12,8},{9,1... | collective-permute-start | bytes 14155784 | tf_op jit(solution)/shard_map/ppermute | solution.py:64
  185.0 17.7 %collective-permute-start.21 = (bf16[128,1536]{1,0:T(8,128)(2,1)}, bf16[128,1536]{1,0:T(8,128)(2,1)}, u32[]{:S(2)}, u32[]{:S(2)}) collective-permute-start(bf16[128,1536]{1,0:T(8,128)(2,1)} %get-tuple-element.40), channel_id=1, source_target_pairs={{0,8},{4,36},{8,16},{12,44},{16,24},{20,52},{24,0},{28,60},{32,40}... | collective-permute-start | bytes 1179656 | tf_op jit(solution)/shard_map/ppermute | solution.py:60
  185.0 18.7 %collective-permute-start.22 = (bf16[128,1536]{1,0:T(8,128)(2,1)}, bf16[128,1536]{1,0:T(8,128)(2,1)}, u32[]{:S(2)}, u32[]{:S(2)}) collective-permute-start(bf16[128,1536]{1,0:T(8,128)(2,1)} %get-tuple-element.40), channel_id=1, source_target_pairs={{0,24},{4,100},{8,0},{12,108},{16,8},{20,116},{24,16},{28,124},{32... | collective-permute-start | bytes 1179656 | tf_op jit(solution)/shard_map/ppermute | solution.py:60
  203.7 11.1 %collective-permute-start.23 = (bf16[64,1536]{1,0:T(8,128)(2,1)S(1)}, bf16[64,1536]{1,0:T(8,128)(2,1)S(1)}, u32[]{:S(2)}, u32[]{:S(2)}) collective-permute-start(bf16[64,1536]{1,0:T(8,128)(2,1)S(1)} %slice.648), channel_id=1, source_target_pairs={{0,8},{4,36},{8,16},{12,44},{16,24},{20,52},{24,0},{28,60},{32,40}... | collective-permute-start | bytes 589832 | tf_op jit(solution)/shard_map/ppermute | solution.py:60
  204.7 10.9 %collective-permute-start.24 = (bf16[64,1536]{1,0:T(8,128)(2,1)S(1)}, bf16[64,1536]{1,0:T(8,128)(2,1)S(1)}, u32[]{:S(2)}, u32[]{:S(2)}) collective-permute-start(bf16[64,1536]{1,0:T(8,128)(2,1)S(1)} %slice.649), channel_id=1, source_target_pairs={{0,24},{4,100},{8,0},{12,108},{16,8},{20,116},{24,16},{28,124},{32... | collective-permute-start | bytes 589832 | tf_op jit(solution)/shard_map/ppermute | solution.py:60
  216.3 22.3 %collective-permute-start.25 = (bf16[512,1536]{1,0:T(8,128)(2,1)}, bf16[512,1536]{1,0:T(8,128)(2,1)}, u32[]{:S(2)}, u32[]{:S(2)}) collective-permute-start(bf16[512,1536]{1,0:T(8,128)(2,1)} %get-tuple-element.146), channel_id=1, source_target_pairs={{0,32},{4,12},{8,40},{12,20},{16,48},{20,28},{24,56},{28,4},{32,64... | collective-permute-start | bytes 4718600 | tf_op jit(solution)/shard_map/ppermute | solution.py:60
  216.6 25.0 %collective-permute-start.26 = (bf16[512,1536]{1,0:T(8,128)(2,1)}, bf16[512,1536]{1,0:T(8,128)(2,1)}, u32[]{:S(2)}, u32[]{:S(2)}) collective-permute-start(bf16[512,1536]{1,0:T(8,128)(2,1)} %get-tuple-element.146), channel_id=1, source_target_pairs={{0,96},{4,28},{8,104},{12,4},{16,112},{20,12},{24,120},{28,20},{32... | collective-permute-start | bytes 4718600 | tf_op jit(solution)/shard_map/ppermute | solution.py:60
  239.8 13.3 %collective-permute-start.27 = (bf16[256,1536]{1,0:T(8,128)(2,1)S(1)}, bf16[256,1536]{1,0:T(8,128)(2,1)S(1)}, u32[]{:S(2)}, u32[]{:S(2)}) collective-permute-start(bf16[256,1536]{1,0:T(8,128)(2,1)S(1)} %slice.650), channel_id=1, source_target_pairs={{0,32},{4,12},{8,40},{12,20},{16,48},{20,28},{24,56},{28,4},{32,64... | collective-permute-start | bytes 2359304 | tf_op jit(solution)/shard_map/ppermute | solution.py:60
  243.4 13.0 %collective-permute-start.28 = (bf16[256,1536]{1,0:T(8,128)(2,1)S(1)}, bf16[256,1536]{1,0:T(8,128)(2,1)S(1)}, u32[]{:S(2)}, u32[]{:S(2)}) collective-permute-start(bf16[256,1536]{1,0:T(8,128)(2,1)S(1)} %slice.651), channel_id=1, source_target_pairs={{0,96},{4,28},{8,104},{12,4},{16,112},{20,12},{24,120},{28,20},{32... | collective-permute-start | bytes 2359304 | tf_op jit(solution)/shard_map/ppermute | solution.py:60
  298.7 13.7 %collective-permute-start.40 = (bf16[256,1536]{1,0:T(8,128)(2,1)S(1)}, bf16[256,1536]{1,0:T(8,128)(2,1)S(1)}, u32[]{:S(2)}, u32[]{:S(2)}) collective-permute-start(bf16[256,1536]{1,0:T(8,128)(2,1)S(1)} %get-tuple-element.51), channel_id=1, source_target_pairs={{0,32},{4,12},{8,40},{12,20},{16,48},{20,28},{24,56},{28,4},{32,64... | collective-permute-start | bytes 2359304 | tf_op jit(solution)/shard_map/ppermute | solution.py:60
  299.1 13.3 %collective-permute-start.42 = (bf16[256,1536]{1,0:T(8,128)(2,1)S(1)}, bf16[256,1536]{1,0:T(8,128)(2,1)S(1)}, u32[]{:S(2)}, u32[]{:S(2)}) collective-permute-start(bf16[256,1536]{1,0:T(8,128)(2,1)S(1)} %get-tuple-element.52), channel_id=1, source_target_pairs={{0,96},{4,28},{8,104},{12,4},{16,112},{20,12},{24,120},{28,20},{32... | collective-permute-start | bytes 2359304 | tf_op jit(solution)/shard_map/ppermute | solution.py:60
  302.6 14.2 %collective-permute-start.19 = (bf16[128,1536]{1,0:T(8,128)(2,1)}, bf16[128,1536]{1,0:T(8,128)(2,1)S(1)}, u32[]{:S(2)}, u32[]{:S(2)}) collective-permute-start(bf16[128,1536]{1,0:T(8,128)(2,1)} %get-tuple-element.40), channel_id=1, source_target_pairs={{0,4},{4,0},{1,5},{5,1},{2,6},{6,2},{3,7},{7,3},{8,12},{12,8},{9,1... | collective-permute-start | bytes 1179656 | tf_op jit(solution)/shard_map/ppermute | solution.py:64
  313.0 21.8 %collective-permute-start.41 = (bf16[512,1536]{1,0:T(8,128)(2,1)S(1)}, bf16[512,1536]{1,0:T(8,128)(2,1)S(1)}, u32[]{:S(2)}, u32[]{:S(2)}) collective-permute-start(bf16[512,1536]{1,0:T(8,128)(2,1)S(1)} %pad_maximum_fusion.9), channel_id=1, source_target_pairs={{0,32},{4,12},{8,40},{12,20},{16,48},{20,28},{24,56},{28,4},{32,64... | collective-permute-start | bytes 4718600 | tf_op jit(solution)/shard_map/ppermute | solution.py:60
  314.6 22.0 %collective-permute-start.43 = (bf16[512,1536]{1,0:T(8,128)(2,1)S(1)}, bf16[512,1536]{1,0:T(8,128)(2,1)S(1)}, u32[]{:S(2)}, u32[]{:S(2)}) collective-permute-start(bf16[512,1536]{1,0:T(8,128)(2,1)S(1)} %pad_maximum_fusion.10), channel_id=1, source_target_pairs={{0,96},{4,28},{8,104},{12,4},{16,112},{20,12},{24,120},{28,20},{32... | collective-permute-start | bytes 4718600 | tf_op jit(solution)/shard_map/ppermute | solution.py:60
  363.0 195.0 %reduce-scatter.5.cloned.1.call-start = ((), (), s32[]{:S(2)}) async-start(), calls=%async_computation.6 | async-start | bytes 5898240 | tf_op jit(solution)/shard_map/reduce_scatter | solution.py:564
  378.9 76.8 %collective-permute-start.66 = (bf16[1536,1536]{1,0:T(8,128)(2,1)}, bf16[1536,1536]{1,0:T(8,128)(2,1)}, u32[]{:S(2)}, u32[]{:S(2)}) collective-permute-start(bf16[1536,1536]{1,0:T(8,128)(2,1)} %broadcast_select_fusion), channel_id=1, source_target_pairs={{0,4},{4,0},{1,5},{5,1},{2,6},{6,2},{3,7},{7,3},{8,12},{12,8},{9,1... | collective-permute-start | bytes 14155784 | tf_op jit(solution)/shard_map/ppermute | solution.py:64
  398.6 37.4 %collective-permute-start.30 = (bf16[256,1536]{1,0:T(8,128)(2,1)}, bf16[256,1536]{1,0:T(8,128)(2,1)}, u32[]{:S(2)}, u32[]{:S(2)}) collective-permute-start(bf16[256,1536]{1,0:T(8,128)(2,1)} %get-tuple-element.57), channel_id=1, source_target_pairs={{0,32},{4,12},{8,40},{12,20},{16,48},{20,28},{24,56},{28,4},{32,64... | collective-permute-start | bytes 2359304 | tf_op jit(solution)/shard_map/ppermute | solution.py:60
  400.1 35.9 %collective-permute-start.32 = (bf16[256,1536]{1,0:T(8,128)(2,1)}, bf16[256,1536]{1,0:T(8,128)(2,1)}, u32[]{:S(2)}, u32[]{:S(2)}) collective-permute-start(bf16[256,1536]{1,0:T(8,128)(2,1)} %get-tuple-element.58), channel_id=1, source_target_pairs={{0,96},{4,28},{8,104},{12,4},{16,112},{20,12},{24,120},{28,20},{32... | collective-permute-start | bytes 2359304 | tf_op jit(solution)/shard_map/ppermute | solution.py:60
  432.6 17.0 %collective-permute-start.49 = (bf16[512,512]{1,0:T(8,128)(2,1)S(1)}, bf16[512,512]{1,0:T(8,128)(2,1)S(1)}, u32[]{:S(2)}, u32[]{:S(2)}) collective-permute-start(bf16[512,512]{1,0:T(8,128)(2,1)S(1)} %get-tuple-element.71), channel_id=1, source_target_pairs={{0,32},{4,12},{8,40},{12,20},{16,48},{20,28},{24,56},{28,4},{32,64... | collective-permute-start | bytes 1572872 | tf_op jit(solution)/shard_map/ppermute | solution.py:60
  433.0 16.6 %collective-permute-start.51 = (bf16[512,512]{1,0:T(8,128)(2,1)S(1)}, bf16[512,512]{1,0:T(8,128)(2,1)S(1)}, u32[]{:S(2)}, u32[]{:S(2)}) collective-permute-start(bf16[512,512]{1,0:T(8,128)(2,1)S(1)} %get-tuple-element.72), channel_id=1, source_target_pairs={{0,96},{4,28},{8,104},{12,4},{16,112},{20,12},{24,120},{28,20},{32... | collective-permute-start | bytes 1572872 | tf_op jit(solution)/shard_map/ppermute | solution.py:60
  439.5 64.4 %collective-permute-start.31 = (bf16[512,1536]{1,0:T(8,128)(2,1)}, bf16[512,1536]{1,0:T(8,128)(2,1)}, u32[]{:S(2)}, u32[]{:S(2)}) collective-permute-start(bf16[512,1536]{1,0:T(8,128)(2,1)} %pad_maximum_fusion.5), channel_id=1, source_target_pairs={{0,32},{4,12},{8,40},{12,20},{16,48},{20,28},{24,56},{28,4},{32,64... | collective-permute-start | bytes 4718600 | tf_op jit(solution)/shard_map/ppermute | solution.py:60
  451.4 26.4 %collective-permute-start.50 = (bf16[1024,512]{1,0:T(8,128)(2,1)S(1)}, bf16[1024,512]{1,0:T(8,128)(2,1)}, u32[]{:S(2)}, u32[]{:S(2)}) collective-permute-start(bf16[1024,512]{1,0:T(8,128)(2,1)S(1)} %pad_maximum_fusion.11), channel_id=1, source_target_pairs={{0,32},{4,12},{8,40},{12,20},{16,48},{20,28},{24,56},{28,4},{32,64... | collective-permute-start | bytes 3145736 | tf_op jit(solution)/shard_map/ppermute | solution.py:60
  452.6 25.2 %collective-permute-start.52 = (bf16[1024,512]{1,0:T(8,128)(2,1)}, bf16[1024,512]{1,0:T(8,128)(2,1)S(1)}, u32[]{:S(2)}, u32[]{:S(2)}) collective-permute-start(bf16[1024,512]{1,0:T(8,128)(2,1)} %pad_maximum_fusion.12), channel_id=1, source_target_pairs={{0,96},{4,28},{8,104},{12,4},{16,112},{20,12},{24,120},{28,20},{32... | collective-permute-start | bytes 3145736 | tf_op jit(solution)/shard_map/ppermute | solution.py:60
  483.3 23.3 %collective-permute-start.33 = (bf16[512,1536]{1,0:T(8,128)(2,1)S(1)}, bf16[512,1536]{1,0:T(8,128)(2,1)S(1)}, u32[]{:S(2)}, u32[]{:S(2)}) collective-permute-start(bf16[512,1536]{1,0:T(8,128)(2,1)S(1)} %pad_maximum_fusion.6), channel_id=1, source_target_pairs={{0,96},{4,28},{8,104},{12,4},{16,112},{20,12},{24,120},{28,20},{32... | collective-permute-start | bytes 4718600 | tf_op jit(solution)/shard_map/ppermute | solution.py:60
  500.3 10.3 %collective-permute-start.58 = (bf16[192,1280]{1,0:T(8,128)(2,1)S(1)}, bf16[192,1280]{1,0:T(8,128)(2,1)S(1)}, u32[]{:S(2)}, u32[]{:S(2)}) collective-permute-start(bf16[192,1280]{1,0:T(8,128)(2,1)S(1)} %get-tuple-element.77), channel_id=1, source_target_pairs={{0,32},{4,12},{8,40},{12,20},{16,48},{20,28},{24,56},{28,4},{32,64... | collective-permute-start | bytes 1474568 | tf_op jit(solution)/shard_map/ppermute | solution.py:60
  500.6 11.2 %collective-permute-start.60 = (bf16[192,1280]{1,0:T(8,128)(2,1)S(1)}, bf16[192,1280]{1,0:T(8,128)(2,1)S(1)}, u32[]{:S(2)}, u32[]{:S(2)}) collective-permute-start(bf16[192,1280]{1,0:T(8,128)(2,1)S(1)} %get-tuple-element.78), channel_id=1, source_target_pairs={{0,96},{4,28},{8,104},{12,4},{16,112},{20,12},{24,120},{28,20},{32... | collective-permute-start | bytes 1474568 | tf_op jit(solution)/shard_map/ppermute | solution.py:60
  512.1 17.9 %collective-permute-start.59 = (bf16[384,1280]{1,0:T(8,128)(2,1)S(1)}, bf16[384,1280]{1,0:T(8,128)(2,1)S(1)}, u32[]{:S(2)}, u32[]{:S(2)}) collective-permute-start(bf16[384,1280]{1,0:T(8,128)(2,1)S(1)} %pad_maximum_fusion.17), channel_id=1, source_target_pairs={{0,32},{4,12},{8,40},{12,20},{16,48},{20,28},{24,56},{28,4},{32,64... | collective-permute-start | bytes 2949128 | tf_op jit(solution)/shard_map/ppermute | solution.py:60
  512.3 17.7 %collective-permute-start.61 = (bf16[384,1280]{1,0:T(8,128)(2,1)S(1)}, bf16[384,1280]{1,0:T(8,128)(2,1)S(1)}, u32[]{:S(2)}, u32[]{:S(2)}) collective-permute-start(bf16[384,1280]{1,0:T(8,128)(2,1)S(1)} %pad_maximum_fusion.18), channel_id=1, source_target_pairs={{0,96},{4,28},{8,104},{12,4},{16,112},{20,12},{24,120},{28,20},{32... | collective-permute-start | bytes 2949128 | tf_op jit(solution)/shard_map/ppermute | solution.py:60
  520.5 85.1 %collective-permute-start.20 = (f32[128,1536]{1,0:T(8,128)}, f32[128,1536]{1,0:T(8,128)}, u32[]{:S(2)}, u32[]{:S(2)}) collective-permute-start(f32[128,1536]{1,0:T(8,128)} %constant_dynamic-slice_fusion.4), channel_id=1, source_target_pairs={{0,4},{4,0},{1,5},{5,1},{2,6},{6,2},{3,7},{7,3},{8,12},{12,8},{9,1... | collective-permute-start | bytes 2359304 | tf_op jit(solution)/shard_map/ppermute | solution.py:64
  526.9 78.7 %collective-permute-start.35 = (bf16[128,1536]{1,0:T(8,128)(2,1)}, bf16[128,1536]{1,0:T(8,128)(2,1)}, u32[]{:S(2)}, u32[]{:S(2)}) collective-permute-start(bf16[128,1536]{1,0:T(8,128)(2,1)} %pad_maximum_fusion.25), channel_id=1, source_target_pairs={{0,8},{4,36},{8,16},{12,44},{16,24},{20,52},{24,0},{28,60},{32,40}... | collective-permute-start | bytes 1179656 | tf_op jit(solution)/shard_map/ppermute | solution.py:60
  530.5 9.5 %collective-permute-start.62 = (bf16[48,1280]{1,0:T(8,128)(2,1)S(1)}, bf16[48,1280]{1,0:T(8,128)(2,1)S(1)}, u32[]{:S(2)}, u32[]{:S(2)}) collective-permute-start(bf16[48,1280]{1,0:T(8,128)(2,1)S(1)} %get-tuple-element.106), channel_id=1, source_target_pairs={{0,8},{4,36},{8,16},{12,44},{16,24},{20,52},{24,0},{28,60},{32,40}... | collective-permute-start | bytes 368648 | tf_op jit(solution)/shard_map/ppermute | solution.py:60
  550.0 18.5 %all-to-all-start.1 = ((bf16[8,12,3584]{2,1,0:T(8,128)(2,1)}), bf16[8,12,3584]{2,1,0:T(8,128)(2,1)}, u32[]{:S(2)}, u32[]{:S(2)}) async-start(bf16[8,12,3584]{2,1,0:T(8,128)(2,1)} %reshape.298), calls=%async_computation.2 | async-start | bytes 1835008 | tf_op jit(solution)/shard_map/all_to_all | solution.py:613
  575.6 30.0 %collective-permute-start.37 = (bf16[128,1536]{1,0:T(8,128)(2,1)}, bf16[128,1536]{1,0:T(8,128)(2,1)}, u32[]{:S(2)}, u32[]{:S(2)}) collective-permute-start(bf16[128,1536]{1,0:T(8,128)(2,1)} %pad_maximum_fusion.26), channel_id=1, source_target_pairs={{0,24},{4,100},{8,0},{12,108},{16,8},{20,116},{24,16},{28,124},{32... | collective-permute-start | bytes 1179656 | tf_op jit(solution)/shard_map/ppermute | solution.py:60
  (121 other events, 1647.7 us)
Sparse Core Ops, SparseCore 0:
  10.3 58.0 all-gather.7
  71.1 77.0 all-gather.5
  150.3 66.9 all-gather.9
  363.1 87.2 reduce-scatter.2
  462.5 50.1 reduce-scatter.4

commit v2 on v1

v2 whole, which is shorter than its diff:
```python
import functools

import jax
import jax.numpy as jnp
from jax import lax
from jax.experimental import pallas as pl
from jax.experimental.layout import Layout, with_layout_constraint
from jax.experimental.pallas import tpu as pltpu
from jax.sharding import Mesh
from jax.sharding import PartitionSpec as P

HEADS = 12
KV_HEADS = 4
HEAD_DIM = 128
GROUP = HEADS // KV_HEADS
EXPERT_FF = 512
SHARED_FF = 1024
TOP = 6
STEP = 10

EPS_NORM = 1e-05
CLIP_NORM = 1.0
FIRST_DECAY = 0.9
SECOND_DECAY = 0.95
ADAM_EPS = 1e-08
WEIGHT_DECAY = 0.1
MATRIX_RATE = 0.05
GAIN_RATE = 0.6
NEGATIVE = -1e30

QW = HEADS * HEAD_DIM
KW = KV_HEADS * HEAD_DIM
STARTS = (0, QW, QW + KW, QW + 2 * KW, 2 * QW + 2 * KW, 2 * QW + 2 * KW + SHARED_FF, 2 * QW + 2 * KW + 2 * SHARED_FF)
WIDTHS = (QW, KW, KW, QW, SHARED_FF, SHARED_FF, SHARED_FF)
HALF_WIDTHS = tuple(w // 2 for w in WIDTHS)
HALF_COLS = sum(HALF_WIDTHS)
QKV_HALF = sum(HALF_WIDTHS[:3])
QKVO_HALF = sum(HALF_WIDTHS[:4])
SHARED_PART = SHARED_FF // 8
MINE = QKVO_HALF + 3 * SHARED_PART
HEADS_HALF = HEADS // 2
KV_HALF = KV_HEADS // 2

CHIPS = ("y", "x")
CTX = ("y", "x", "core")
DEPTH = ("wt", "seq")
COLUMN = ("core", "wt", "seq")
ALL = CTX + DEPTH
BF = jnp.bfloat16
F32 = jnp.float32
LOG2E = 1.4426950408889634
MIB = 1 << 20
CHUNK = 512


def turn(v, phase, step):
    pairs = []
    for y in range(4):
        for x in range(4):
            for core in range(2):
                along_x = (phase == 1) == (core == 0)
                ty, tx = (y, (x + step) % 4) if along_x else ((y + step) % 4, x)
                pairs.append(((y * 4 + x) * 2 + core, (ty * 4 + tx) * 2 + core))
    return lax.ppermute(v, CTX, pairs)


def swap(v):
    return lax.ppermute(v, "core", [(0, 1), (1, 0)])


def ring_pieces(v, phase):
    return [v, turn(v, phase, 1), turn(v, phase, -1), turn(v, phase, 2)]


def gather_plane(v, wait=None):
    v = jnp.concatenate(ring_pieces(v, 1), axis=0)
    return ring_pieces(v if wait is None else v + wait.astype(v.dtype), 2)


def ring_sum(pieces, phase):
    own, left, right, far = pieces
    terms = [own, turn(left, phase, -1), turn(right, phase, 1), turn(far, phase, 2)]
    return sum(t.astype(F32) for t in terms)


def sum_plane(pieces, wait=0.0):
    g = (ring_sum(pieces, 2) + wait).astype(BF)
    rows = g.shape[0] // 4
    return ring_sum([g[k * rows : (k + 1) * rows] for k in range(4)], 1)


def zero_after(v):
    return jnp.minimum(jnp.abs(v[(0,) * v.ndim].astype(F32)), 0.0)


def block_chips(iy, ix, first_core):
    offsets = jnp.array([0, 3, 1, 2], jnp.int32)
    outer, inner = jnp.repeat(offsets, 4), jnp.tile(offsets, 4)
    y = (iy + jnp.where(first_core, outer, inner)) % 4
    x = (ix + jnp.where(first_core, inner, outer)) % 4
    return y * 4 + x


def row_major(v):
    return with_layout_constraint(v, Layout(tuple(range(v.ndim))))


def pieces_of(refs, rows):
    return [(refs[b // 4], b % 4 * rows) for b in range(16)]


def spread_kernel(dense, out):
    for core in range(2):
        for z in range(4):
            at = 0
            for k, (start, width) in enumerate(zip(STARTS, HALF_WIDTHS, strict=True)):
                first = start + core * width
                if k >= 4:
                    width //= 4
                    first += z * width
                out[core * 4 + z, :, at : at + width] = dense[:, first : first + width].astype(BF)
                at += width


def spread(dense):
    return pl.pallas_call(
        spread_kernel,
        out_shape=jax.ShapeDtypeStruct((8, dense.shape[0], MINE), BF),
        compiler_params=pltpu.CompilerParams(vmem_limit_bytes=8 * MIB),
    )(dense)


def project_kernel(chips, h, p0, p1, p2, p3, query, kv, weights, small, held, small_held, sems, out_sem):
    extra = small_held.shape[0] // 16
    rows = p0.shape[0] // 4 - extra
    needed, others = [], []
    for b, (ref, row) in enumerate(pieces_of((p0, p1, p2, p3), rows + extra)):
        to = pl.ds(pl.multiple_of(chips[b] * rows, rows), rows)
        needed.append(
            pltpu.make_async_copy(ref.at[pl.ds(row, rows), :], held.at[to, :], sems.at[b, 0])
        )
        others.append(
            pltpu.make_async_copy(
                ref.at[pl.ds(row + rows, extra), :],
                small_held.at[pl.ds(b * extra, extra), :],
                sems.at[b, 1],
            )
        )
    for copy in needed + others:
        copy.start()
    for copy in needed:
        copy.wait()
    out = pltpu.make_async_copy(held, weights, out_sem.at[0])
    out.start()
    split = query.shape[1]
    query[...] = dot(h[...], held[:, :split]).astype(BF)
    kv[...] = dot(h[...], held[:, split : split + kv.shape[1]]).astype(BF)
    for b, copy in enumerate(others):
        copy.wait()
        small[b] = small_held[b * extra : b * extra + 8, :].astype(F32)
    out.wait()


def project(chips, h, pieces, extra):
    rows, width = h.shape
    cols = pieces[0].shape[1]
    anywhere, vectors = pl.BlockSpec(memory_space=pl.ANY), pl.BlockSpec(memory_space=pltpu.VMEM)
    return pl.pallas_call(
        project_kernel,
        in_specs=[pl.BlockSpec(memory_space=pltpu.SMEM), vectors] + [anywhere] * 4,
        out_specs=[vectors, vectors, anywhere, vectors],
        out_shape=[
            jax.ShapeDtypeStruct((rows, HALF_WIDTHS[0]), BF),
            jax.ShapeDtypeStruct((rows, QKV_HALF - HALF_WIDTHS[0]), BF),
            jax.ShapeDtypeStruct((width, cols), BF),
            jax.ShapeDtypeStruct((16, 8, cols), F32),
        ],
        scratch_shapes=[
            pltpu.VMEM((width, cols), BF),
            pltpu.VMEM((16 * extra, cols), BF),
            pltpu.SemaphoreType.DMA((16, 2)),
            pltpu.SemaphoreType.DMA((1,)),
        ],
        cost_estimate=pl.CostEstimate(
            flops=2 * rows * width * QKV_HALF, bytes_accessed=16 * MIB, transcendentals=0
        ),
        compiler_params=pltpu.CompilerParams(vmem_limit_bytes=18 * MIB),
    )(chips, h, *pieces)


def shared_kernel(h_ref, up_ref, w_ref, out_ref, dh_ref, grad_ref):
    @pl.when(pl.program_id(0) == 0)
    def _():
        out_ref[...] = jnp.zeros_like(out_ref)
        dh_ref[...] = jnp.zeros_like(dh_ref)

    h, upstream = h_ref[...], up_ref[...]
    w_gu, w_d = w_ref[:, : 2 * SHARED_PART], w_ref[:, 2 * SHARED_PART :]
    pre = dot(h, w_gu)
    gate, up = pre[:, :SHARED_PART], pre[:, SHARED_PART:]
    act, deriv = silu_parts(gate)
    mid = (act * up).astype(BF)
    d_mid = dot(upstream, w_d)
    d_pre = jnp.concatenate([(d_mid * up * deriv).astype(BF), (d_mid * act).astype(BF)], axis=1)
    out_ref[...] += times_transposed(mid, w_d)
    dh_ref[...] += times_transposed(d_pre, w_gu)
    grad_ref[:, : 2 * SHARED_PART] = transposed_times(h, d_pre).astype(BF)
    grad_ref[:, 2 * SHARED_PART :] = transposed_times(upstream, mid).astype(BF)


def shared_expert(h, upstream, weights):
    rows, width = h.shape
    cols = weights.shape[1]
    whole = pl.BlockSpec((rows, width), lambda z: (0, 0))
    part = pl.BlockSpec((width, cols), lambda z: (z, 0))
    return pl.pallas_call(
        shared_kernel,
        grid=(4,),
        in_specs=[whole, whole, part],
        out_specs=[whole, whole, part],
        out_shape=[
            jax.ShapeDtypeStruct((rows, width), F32),
            jax.ShapeDtypeStruct((rows, width), F32),
            jax.ShapeDtypeStruct(weights.shape, BF),
        ],
        cost_estimate=pl.CostEstimate(
            flops=6 * rows * width * cols * 4, bytes_accessed=14 * MIB, transcendentals=rows * 512
        ),
        compiler_params=pltpu.CompilerParams(vmem_limit_bytes=18 * MIB),
    )(h, upstream, weights)


def by_visibility(bounds, first, second, length, run):
    start_low, start_high, low, high = (bounds[k] for k in range(4))
    last = length - 1

    def whole(at):
        return (at >= start_high) & (at + last <= low)

    def some(at):
        return (at + last >= start_low) & (at <= high)

    all_seen = whole(first) & whole(second)
    any_seen = some(first) | some(second)
    pl.when(all_seen)(lambda: run(False))
    pl.when(any_seen & jnp.logical_not(all_seen))(lambda: run(True))


def seen(query_range, first, second, length):
    spots = lax.broadcasted_iota(jnp.int32, (length, query_range.shape[1]), 0)
    parts = []
    for at in (first, second):
        parts.append(
            (spots >= query_range[0:1, :] - at) & (spots <= query_range[1:2, :] - at)
        )
    return parts


def attend_kernel(scale, chips, bounds, ranges, q_ref, p0, p1, p2, p3, out_ref, lse_ref, acc, top, total):
    acc[...] = jnp.zeros_like(acc)
    total[...] = jnp.zeros_like(total)
    top[...] = jnp.full_like(top, -jnp.inf)
    rows = q_ref.shape[0]
    places = pieces_of((p0, p1, p2, p3), rows)
    for b in range(0, 16, 2):
        ref, row = places[b]
        block = pl.ds(row, 2 * rows)
        first, second = chips[b] * rows, chips[b + 1] * rows

        def run(masked, ref=ref, block=block, first=first, second=second):
            if masked:
                visible = jnp.concatenate(seen(ranges[...], first, second, rows), axis=0)
            for head in range(HEADS_HALF):
                kv_head = head // GROUP
                cols = slice(head * HEAD_DIM, (head + 1) * HEAD_DIM)
                k_at, v_at = kv_head * HEAD_DIM, (KV_HALF + kv_head) * HEAD_DIM
                key = ref[block, k_at : k_at + HEAD_DIM]
                value = ref[block, v_at : v_at + HEAD_DIM]
                scores = times_transposed(key, q_ref[:, cols]) * (scale * LOG2E)
                if masked:
                    scores = jnp.where(visible, scores, NEGATIVE)
                before = top[head : head + 1, :]
                now = jnp.maximum(before, jnp.max(scores, axis=0, keepdims=True))
                expo = jnp.exp2(scores - now)
                fade = jnp.exp2(before - now)
                top[head : head + 1, :] = now
                total[head : head + 1, :] = total[head : head + 1, :] * fade + jnp.sum(
                    expo, axis=0, keepdims=True
                )
                acc[cols, :] = acc[cols, :] * fade + transposed_times(value, expo.astype(BF))

        by_visibility(bounds, first, second, rows, run)
    for head in range(HEADS_HALF):
        cols = slice(head * HEAD_DIM, (head + 1) * HEAD_DIM)
        out_ref[:, cols] = (acc[cols, :] / total[head : head + 1, :]).T
    lse_ref[...] = top[...] + jnp.log2(total[...])


def attend(chips, bounds, ranges, query, pieces, scale):
    rows, cols = query.shape
    keys = 16 * rows
    in_scalars, in_vectors = pl.BlockSpec(memory_space=pltpu.SMEM), pl.BlockSpec(memory_space=pltpu.VMEM)
    return pl.pallas_call(
        functools.partial(attend_kernel, scale),
        in_specs=[in_scalars] * 2 + [in_vectors] * 6,
        out_specs=[in_vectors] * 2,
        out_shape=[
            jax.ShapeDtypeStruct((rows, cols), F32),
            jax.ShapeDtypeStruct((8, rows), F32),
        ],
        scratch_shapes=[
            pltpu.VMEM((cols, rows), F32),
            pltpu.VMEM((8, rows), F32),
            pltpu.VMEM((8, rows), F32),
        ],
        cost_estimate=pl.CostEstimate(
            flops=4 * rows * cols * keys, bytes_accessed=8 * MIB, transcendentals=rows * keys * 6
        ),
        compiler_params=pltpu.CompilerParams(vmem_limit_bytes=18 * MIB),
    )(chips, bounds, ranges, query, *pieces)


def attend_back_kernel(
    scale, chips, bounds, ranges, q_ref, do_ref, o_ref, lse_ref, p0, p1, p2, p3,
    dq_ref, g0, g1, g2, g3, acc, delta
):
    acc[...] = jnp.zeros_like(acc)
    for head in range(HEADS_HALF):
        cols = slice(head * HEAD_DIM, (head + 1) * HEAD_DIM)
        shared = do_ref[:, cols].astype(F32) * o_ref[:, cols]
        delta[head : head + 1, :] = jnp.sum(shared.T, axis=0, keepdims=True)
    rows = q_ref.shape[0]
    places = pieces_of((p0, p1, p2, p3), rows)
    grads = pieces_of((g0, g1, g2, g3), rows)
    for b in range(0, 16, 2):
        ref, row = places[b]
        out = grads[b][0]
        block = pl.ds(row, 2 * rows)
        first, second = chips[b] * rows, chips[b + 1] * rows
        out[block, :] = jnp.zeros((2 * rows, out.shape[1]), BF)

        def run(masked, ref=ref, out=out, block=block, first=first, second=second):
            if masked:
                visible = jnp.concatenate(seen(ranges[...], first, second, rows), axis=0)
            for kv_head in range(KV_HALF):
                k_at, v_at = kv_head * HEAD_DIM, (KV_HALF + kv_head) * HEAD_DIM
                key = ref[block, k_at : k_at + HEAD_DIM]
                value = ref[block, v_at : v_at + HEAD_DIM]
                key_grad = jnp.zeros(key.shape, F32)
                value_grad = jnp.zeros(key.shape, F32)
                for member in range(GROUP):
                    head = kv_head * GROUP + member
                    cols = slice(head * HEAD_DIM, (head + 1) * HEAD_DIM)
                    query, upstream = q_ref[:, cols], do_ref[:, cols]
                    scores = times_transposed(key, query) * (scale * LOG2E)
                    if masked:
                        scores = jnp.where(visible, scores, NEGATIVE)
                    chances = jnp.exp2(scores - lse_ref[head : head + 1, :])
                    inner = times_transposed(value, upstream)
                    grad_scores = (chances * (inner - delta[head : head + 1, :])).astype(BF)
                    value_grad += dot(chances.astype(BF), upstream)
                    key_grad += dot(grad_scores, query)
                    acc[cols, :] += transposed_times(key, grad_scores)
                out[block, k_at : k_at + HEAD_DIM] = (key_grad * scale).astype(BF)
                out[block, v_at : v_at + HEAD_DIM] = value_grad.astype(BF)

        by_visibility(bounds, first, second, rows, run)
    for head in range(HEADS_HALF):
        cols = slice(head * HEAD_DIM, (head + 1) * HEAD_DIM)
        dq_ref[:, cols] = (acc[cols, :] * scale).T.astype(BF)


def attend_back(chips, bounds, ranges, query, upstream, out_f, lse, pieces, scale):
    rows, cols = query.shape
    keys = 16 * rows
    in_scalars, in_vectors = pl.BlockSpec(memory_space=pltpu.SMEM), pl.BlockSpec(memory_space=pltpu.VMEM)
    return pl.pallas_call(
        functools.partial(attend_back_kernel, scale),
        in_specs=[in_scalars] * 2 + [in_vectors] * 9,
        out_specs=[in_vectors] * 5,
        out_shape=[jax.ShapeDtypeStruct((rows, cols), BF)]
        + [jax.ShapeDtypeStruct(p.shape, BF) for p in pieces],
        scratch_shapes=[pltpu.VMEM((cols, rows), F32), pltpu.VMEM((8, rows), F32)],
        cost_estimate=pl.CostEstimate(
            flops=10 * rows * cols * keys, bytes_accessed=12 * MIB, transcendentals=rows * keys * 6
        ),
        compiler_params=pltpu.CompilerParams(vmem_limit_bytes=24 * MIB),
    )(chips, bounds, ranges, query, upstream, out_f, lse, *pieces)


def pick_kernel(order, pick, scale, *refs):
    sources, (out, held, ready, in_sems, out_sems) = refs[:4], refs[4:]
    pairs, slots, rows = pick.shape
    half, width = slots // 2, held.shape[1]
    copies = [
        pltpu.make_async_copy(
            sources[p // 2].at[pl.ds(p % 2 * rows, rows), :],
            held.at[pl.ds(p * rows, rows), :],
            in_sems.at[p],
        )
        for p in range(pairs)
    ]
    for copy in copies:
        copy.start()
    sent = []
    for p in range(pairs):
        copies[p].wait()
        for at in range(0, width, CHUNK):
            cols = slice(at, at + CHUNK)
            found = dot(pick[p], held[pl.ds(p * rows, rows), cols])
            if scale is not None:
                found = found * scale[p]
            found = found.astype(BF)
            for e in range(2):
                ready[e, pl.ds(p * half, half), cols] = found[e * half : (e + 1) * half]
        for e in range(2):
            to = pl.ds(p * half, half)
            sent.append(
                pltpu.make_async_copy(ready.at[e, to, :], out.at[e, to, :], out_sems.at[p, e])
            )
            sent[-1].start()
    for copy in sent:
        copy.wait()


def pick_rows(order, pick, scale, sources):
    pairs, slots, rows = pick.shape
    width = sources[0].shape[1]
    vectors, anywhere = pl.BlockSpec(memory_space=pltpu.VMEM), pl.BlockSpec(memory_space=pl.ANY)
    given = [pick] if scale is None else [pick, scale]

    def kernel(order_ref, pick_ref, *refs):
        if scale is None:
            pick_kernel(order_ref, pick_ref, None, *refs)
        else:
            pick_kernel(order_ref, pick_ref, *refs)

    return pl.pallas_call(
        kernel,
        in_specs=[pl.BlockSpec(memory_space=pltpu.SMEM)]
        + [vectors] * len(given)
        + [anywhere] * 4,
        out_specs=anywhere,
        out_shape=jax.ShapeDtypeStruct((2, pairs * slots // 2, width), BF),
        scratch_shapes=[
            pltpu.VMEM((pairs * rows, width), BF),
            pltpu.VMEM((2, pairs * slots // 2, width), BF),
            pltpu.SemaphoreType.DMA((pairs,)),
            pltpu.SemaphoreType.DMA((pairs, 2)),
        ],
        cost_estimate=pl.CostEstimate(
            flops=2 * pairs * slots * rows * width, bytes_accessed=12 * MIB, transcendentals=0
        ),
        compiler_params=pltpu.CompilerParams(vmem_limit_bytes=18 * MIB),
    )(order, *given, *sources)


def unpick_kernel(pick, scale, own, other, o0, o1, o2, o3, held, ready, in_sems, out_sems):
    pairs, slots, rows = pick.shape
    half, width = slots // 2, held.shape[1]
    outs = (o0, o1, o2, o3)
    copies = []
    for p in range(pairs):
        for e, ref in enumerate((own, other)):
            copies.append(
                pltpu.make_async_copy(
                    ref.at[pl.ds(p * half, half), :],
                    held.at[pl.ds(p * slots + e * half, half), :],
                    in_sems.at[p, e],
                )
            )
            copies[-1].start()
    sent = []
    for p in range(pairs):
        copies[2 * p].wait()
        copies[2 * p + 1].wait()
        to = pl.ds(p * rows, rows)
        for at in range(0, width, CHUNK):
            cols = slice(at, at + CHUNK)
            given = held[pl.ds(p * slots, slots), cols]
            if scale is not None:
                given = (given.astype(F32) * scale[p]).astype(BF)
            ready[to, cols] = transposed_times(pick[p], given).astype(BF)
        sent.append(
            pltpu.make_async_copy(
                ready.at[to, :], outs[p // 2].at[pl.ds(p % 2 * rows, rows), :], out_sems.at[p]
            )
        )
        sent[-1].start()
    for copy in sent:
        copy.wait()


def unpick_rows(pick, scale, own, other):
    pairs, slots, rows = pick.shape
    width = own.shape[1]
    vectors, anywhere = pl.BlockSpec(memory_space=pltpu.VMEM), pl.BlockSpec(memory_space=pl.ANY)
    given = [pick] if scale is None else [pick, scale]

    def kernel(pick_ref, *refs):
        if scale is None:
            unpick_kernel(pick_ref, None, *refs)
        else:
            unpick_kernel(pick_ref, *refs)

    return pl.pallas_call(
        kernel,
        in_specs=[vectors] * len(given) + [anywhere] * 2,
        out_specs=[anywhere] * 4,
        out_shape=[jax.ShapeDtypeStruct((pairs * rows // 4, width), BF)] * 4,
        scratch_shapes=[
            pltpu.VMEM((pairs * slots, width), BF),
            pltpu.VMEM((pairs * rows, width), BF),
            pltpu.SemaphoreType.DMA((pairs, 2)),
            pltpu.SemaphoreType.DMA((pairs,)),
        ],
        cost_estimate=pl.CostEstimate(
            flops=2 * pairs * slots * rows * width, bytes_accessed=12 * MIB, transcendentals=0
        ),
        compiler_params=pltpu.CompilerParams(vmem_limit_bytes=18 * MIB),
    )(*given, own, other)


def total_over_all(v):
    v = v + swap(v)
    for axis in ("x", "y"):
        v = v + lax.ppermute(v, axis, [(i, i ^ 1) for i in range(4)])
        v = v + lax.ppermute(v, axis, [(i, i ^ 3) for i in range(4)])
    for axis in DEPTH:
        v = v + lax.ppermute(v, axis, [(0, 1), (1, 0)])
    return v


def silu_parts(values):
    sigmoid_values = jax.nn.sigmoid(values)
    return (values * sigmoid_values, sigmoid_values * (1.0 + values * (1.0 - sigmoid_values)))


def norm_forward(values, gain_row):
    factor = lax.rsqrt(jnp.mean(values * values, axis=-1, keepdims=True) + EPS_NORM)
    normed = values * factor
    return (normed * gain_row, normed, factor)


def norm_backward(upstream, normed, factor, gain_row):
    scaled = upstream * gain_row
    inward = factor * (scaled - normed * jnp.mean(scaled * normed, axis=-1, keepdims=True))
    return (inward, jnp.sum(upstream * normed, axis=0))


def adamw_step(weight, first_moment, second, gradient, step_rate, decay_rate):
    first_moment = FIRST_DECAY * first_moment + (1.0 - FIRST_DECAY) * gradient
    second = SECOND_DECAY * second + (1.0 - SECOND_DECAY) * gradient * gradient
    first_hat = first_moment / (1.0 - FIRST_DECAY**STEP)
    second_hat = second / (1.0 - SECOND_DECAY**STEP)
    weight = weight - step_rate * (
        first_hat / (jnp.sqrt(second_hat) + ADAM_EPS) + decay_rate * weight
    )
    return (weight, first_moment, second)


def dot(left, right):
    return jnp.dot(left, right, preferred_element_type=F32)


def times_transposed(left, right):
    return lax.dot_general(left, right, (((1,), (1,)), ((), ())), preferred_element_type=F32)


def transposed_times(left, right):
    return lax.dot_general(left, right, (((0,), (0,)), ((), ())), preferred_element_type=F32)


def whole_of(halves, quarters):
    columns, at = [], 0
    for width in HALF_WIDTHS[:4]:
        columns += [halves[core][:, at : at + width] for core in range(2)]
        at += width
    part = HALF_WIDTHS[4] // 4
    for k in range(3):
        columns += [
            quarters[core, z][:, k * part : (k + 1) * part] for core in range(2) for z in range(4)
        ]
    return jnp.concatenate(columns, axis=1)


def shards(
    tokens,
    cotangent,
    segment_ids,
    routes,
    gates,
    dense_weights,
    dense_first,
    dense_second,
    expert_weights,
    expert_first,
    expert_second,
    gains,
    gain_first,
    gain_second,
):
    rows = tokens.shape[1]
    width = tokens.shape[2]
    seq_len = rows * 32
    cap = min(rows, 2 * rows * TOP // 32)
    scale = HEAD_DIM ** (-0.5)
    iy, ix, core = lax.axis_index("y"), lax.axis_index("x"), lax.axis_index("core")
    chip = iy * 4 + ix
    first_core = core == 0
    first_of_chip = chip * 2 * rows

    def both_cores(mine, other):
        return jnp.where(
            first_core,
            jnp.concatenate([mine, other], axis=0),
            jnp.concatenate([other, mine], axis=0),
        )

    def of_chip(v):
        return both_cores(v, swap(v))

    def own_rows(v):
        return lax.dynamic_slice_in_dim(v, core * rows, rows, 0)

    def other_rows(v):
        return lax.dynamic_slice_in_dim(v, (1 - core) * rows, rows, 0)

    def summed_for_own(v):
        return own_rows(v) + swap(other_rows(v))

    def three_terms(v):
        high = v.astype(BF)
        rest = v - high.astype(F32)
        mid = rest.astype(BF)
        return [high, mid, (rest - mid.astype(F32)).astype(BF)]

    segments_chip = of_chip(segment_ids[0][None].astype(F32)).reshape(1, 2 * rows)
    digits = jnp.concatenate(
        [jnp.floor(segments_chip / 64.0), segments_chip - 64.0 * jnp.floor(segments_chip / 64.0)],
        axis=0,
    ).astype(BF)
    small = jnp.concatenate(
        [digits.reshape(4, rows), routes[0].T.astype(BF), *three_terms(gates[0].T)], axis=0
    )
    small_rows = small.shape[0]
    extra = 16
    small = jnp.pad(small.reshape(-1), (0, extra * QKVO_HALF - small.size))
    small = small.reshape(extra, QKVO_HALF)

    chip_rows = 8 * dense_weights.shape[0]
    dense_part = lax.all_to_all(spread(dense_weights), COLUMN, 0, 0, tiled=True)
    dense_part = dense_part.reshape(chip_rows, MINE)
    chips = block_chips(iy, ix, first_core)
    qkvo = gather_plane(jnp.concatenate([dense_part[:, :QKVO_HALF], small], axis=0))

    inputs = tokens[0].astype(F32)
    h_one_f, normed_one, factor_one = norm_forward(inputs, gains[0])
    h_one = of_chip(h_one_f.astype(BF))
    upstream = cotangent[0]
    upstream_f = upstream.astype(F32)
    cot_chip = of_chip(upstream)

    expert_low = expert_weights[0].astype(BF)
    expert_own = lax.all_gather(expert_low, DEPTH, axis=0, tiled=True)
    experts = [expert_own, swap(expert_own)]

    query, kv_own, w_qkvo, small_all = project(chips, h_one, qkvo, extra)
    w_qkv, w_o = w_qkvo[:, :QKV_HALF], w_qkvo[:, QKV_HALF:]
    kv_all = gather_plane(kv_own)
    cot_all = gather_plane(upstream, zero_after(kv_all[3]))
    small_all = small_all.reshape(16, -1)[:, : small_rows * rows].reshape(16, small_rows, rows)

    shared_in = dense_part[:, QKVO_HALF:] + zero_after(expert_own).astype(BF)
    shared_quarter = lax.all_gather(shared_in, CHIPS, axis=0, tiled=True)
    shared_all = lax.all_gather(shared_quarter, DEPTH, axis=0, tiled=True)

    places = jnp.arange(width, dtype=jnp.int32)
    source = jnp.repeat(chips, chip_rows) * chip_rows + places % chip_rows
    order = (places[:, None] == source[None, :]).astype(BF)
    h_one_turned = dot(h_one, order).astype(BF)

    segments_all = (small_all[:, :2] * 64.0 + small_all[:, 2:4]).reshape(-1)
    routes_all = small_all[:, 4 : 4 + TOP]
    high, mid_term, low_term = (
        small_all[:, 4 + k * TOP : 4 + (k + 1) * TOP] for k in range(1, 4)
    )
    gates_all = high + mid_term + low_term
    earlier = jnp.triu(jnp.ones((rows, rows), F32), 1).astype(BF)
    picks, gate_slots = [], []
    for local in range(2):
        expert_at = chip * 2 + (core if local == 0 else 1 - core)
        named = routes_all == expert_at.astype(F32)
        hit = jnp.any(named, axis=1)
        gate = jnp.sum(jnp.where(named, gates_all, 0.0), axis=1)
        slot = dot(hit.astype(BF), earlier).astype(jnp.int32)
        slot = (slot.reshape(8, 2, rows) + jnp.array([0, cap], jnp.int32)[:, None]).reshape(8, -1)
        hit, gate = hit.reshape(8, 2 * rows), gate.reshape(8, 2 * rows)
        pick = hit[:, None, :] & (
            slot[:, None, :] == jnp.arange(2 * cap, dtype=jnp.int32)[None, :, None]
        )
        picks.append(pick.astype(BF))
        gate_slots.append(jnp.sum(jnp.where(pick, gate[:, None, :], 0.0), axis=2, keepdims=True))
    pick = jnp.concatenate(picks, axis=1)
    gate_slot = jnp.concatenate(gate_slots, axis=1)

    query_spots = first_of_chip + jnp.arange(2 * rows, dtype=jnp.int32)
    run_start = jnp.sum(
        (segments_all[None, :] < segments_chip.reshape(-1, 1)).astype(jnp.int32), axis=1
    )
    ranges = jnp.concatenate(
        [run_start[None], query_spots[None], jnp.zeros((6, 2 * rows), jnp.int32)], axis=0
    )
    bounds = jnp.stack([run_start[0], run_start[-1], query_spots[0], query_spots[-1]])
    attn_f, lse = attend(chips, bounds, ranges, query, kv_all, scale)
    attn = (attn_f + (zero_after(cot_all[1]) + zero_after(cot_all[2]))).astype(BF)
    resid = inputs + summed_for_own(times_transposed(attn, w_o))
    h_two_f, normed_two, factor_two = norm_forward(resid, gains[1])
    h_two = h_two_f.astype(BF)

    h_two_all = gather_plane(h_two)
    h_two_chip = of_chip(h_two)
    shared_out, grad_h_shared, shared_grads = shared_expert(h_two_chip, cot_chip, shared_all)
    shared_grads = lax.psum_scatter(shared_grads, DEPTH, scatter_dimension=0, tiled=True)
    d_out_both = pick_rows(chips, pick, gate_slot, cot_all)
    later = (zero_after(shared_out) + zero_after(d_out_both)).astype(jnp.int32)
    x_both = pick_rows(chips + later, pick, None, h_two_all)
    outs, d_xs, expert_grads, down_grads = [], [], [], []
    for local in range(2):
        weights = experts[local]
        x = x_both[local]
        pre = dot(x, weights[:, : 2 * EXPERT_FF])
        gate_pre, up_pre = pre[:, :EXPERT_FF], pre[:, EXPERT_FF:]
        act, deriv = silu_parts(gate_pre)
        mid = (act * up_pre).astype(BF)
        outs.append(times_transposed(mid, weights[:, 2 * EXPERT_FF :]).astype(BF))
        d_out = d_out_both[local]
        d_mid = dot(d_out, weights[:, 2 * EXPERT_FF :])
        d_pre = jnp.concatenate(
            [(d_mid * up_pre * deriv).astype(BF), (d_mid * act).astype(BF)], axis=1
        )
        d_xs.append(times_transposed(d_pre, weights[:, : 2 * EXPERT_FF]).astype(BF))
        expert_grads.append(row_major(transposed_times(x, d_pre).astype(BF)))
        down_grads.append(row_major(transposed_times(d_out, mid).astype(BF)))
    expert_done = sum(zero_after(g) for g in expert_grads + down_grads)
    expert_grads = [
        jnp.concatenate(pair, axis=1) for pair in zip(expert_grads, down_grads, strict=True)
    ]
    grad_h_experts = sum_plane(unpick_rows(pick, None, *d_xs), expert_done)

    expert_local = (expert_grads[0].astype(F32) + swap(expert_grads[1]).astype(F32)).astype(BF)
    expert_grad = lax.psum_scatter(
        row_major(expert_local), DEPTH, scatter_dimension=0, tiled=True
    )
    expert_grad = row_major(expert_grad).astype(F32)

    shared_out = summed_for_own(shared_out)
    grad_h_two = summed_for_own(grad_h_shared) + grad_h_experts
    grad_resid_norm, gain_two_part = norm_backward(grad_h_two, normed_two, factor_two, gains[1])
    grad_resid = upstream_f + grad_resid_norm
    grad_att = of_chip(grad_resid.astype(BF))
    grad_attn = dot(grad_att, w_o).astype(BF)

    grad_query, *kv_terms = attend_back(
        chips, bounds, ranges, query, grad_attn, attn_f, lse, kv_all, scale
    )
    grad_kv = sum_plane(kv_terms).astype(BF)
    grad_qkv = jnp.concatenate([grad_query, grad_kv], axis=1)
    grad_h_one = summed_for_own(times_transposed(grad_qkv, w_qkv))
    grad_input_norm, gain_one_part = norm_backward(grad_h_one, normed_one, factor_one, gains[0])
    input_grad = grad_resid + grad_input_norm

    grads_rest = jnp.concatenate(
        [row_major(transposed_times(grad_att, attn).astype(BF)), shared_grads], axis=1
    )
    rest_sum = lax.psum_scatter(grads_rest, CHIPS, scatter_dimension=0, tiled=True)
    quarter = width // 4
    out_terms = unpick_rows(pick, gate_slot + zero_after(grad_kv), *outs)
    qkv_sum = sum_plane(
        [
            transposed_times(h_one_turned[:, k * quarter : (k + 1) * quarter], grad_qkv).astype(BF)
            for k in range(4)
        ],
        zero_after(out_terms[0]),
    )
    mixture = sum_plane(out_terms)
    block_out = (resid + shared_out + mixture).astype(BF)
    part_sum = jnp.concatenate([qkv_sum.astype(BF), rest_sum], axis=1)
    blocks = lax.all_to_all(
        part_sum.reshape(8, chip_rows // 8, MINE), COLUMN, 0, 0, tiled=True
    ).reshape(2, 4, chip_rows // 8, MINE)
    dense_grad = whole_of(
        jnp.sum(blocks[..., :QKVO_HALF].astype(F32), axis=1), blocks[..., QKVO_HALF:].astype(F32)
    )

    gain_part = jnp.stack([gain_one_part, gain_two_part])
    local_squares = jnp.sum(dense_grad * dense_grad) + jnp.sum(expert_grad * expert_grad)
    gain_tiles = gain_part.size // 128
    packed = jnp.concatenate(
        [
            gain_part.reshape(gain_tiles, 128),
            jnp.broadcast_to(local_squares, (8, 128)),
        ],
        axis=0,
    )
    packed = total_over_all(packed)
    gain_grad = packed[:gain_tiles].reshape(gain_part.shape)
    total_squares = packed[gain_tiles, 0]
    grad_norm = jnp.sqrt(total_squares + jnp.sum(gain_grad * gain_grad))
    clip_factor = jnp.minimum(1.0, CLIP_NORM / (grad_norm + 1e-06))
    dense_new, dense_first_new, dense_second_new = adamw_step(
        dense_weights,
        dense_first,
        dense_second,
        dense_grad * clip_factor,
        MATRIX_RATE,
        WEIGHT_DECAY,
    )
    expert_new, expert_first_new, expert_second_new = adamw_step(
        expert_weights,
        expert_first,
        expert_second,
        expert_grad[None] * clip_factor,
        MATRIX_RATE,
        WEIGHT_DECAY,
    )
    gain_cols = gain_first.shape[1]
    gain_begin = lax.axis_index(ALL) * gain_cols
    gain_slice = lax.dynamic_slice_in_dim(gains, gain_begin, gain_cols, 1)
    gain_grad_slice = lax.dynamic_slice_in_dim(gain_grad, gain_begin, gain_cols, 1)
    gain_new, gain_first_new, gain_second_new = adamw_step(
        gain_slice, gain_first, gain_second, gain_grad_slice * clip_factor, GAIN_RATE, 0.0
    )
    return (
        block_out[None],
        input_grad[None],
        grad_norm,
        dense_new,
        dense_first_new,
        dense_second_new,
        expert_new,
        expert_first_new,
        expert_second_new,
        gain_new,
        gain_first_new,
        gain_second_new,
    )


def solution(mesh):
    fine = Mesh(mesh.devices.reshape(4, 4, 2, 2, 2), ALL)
    sequence = (DEPTH, CTX)
    token = P(*sequence, None)
    dense = P(ALL, None)
    expert = P(CTX, DEPTH, None)
    gain = P(None, ALL)
    return jax.shard_map(
        shards,
        mesh=fine,
        in_specs=(
            token,
            token,
            P(*sequence),
            token,
            token,
            dense,
            dense,
            dense,
            expert,
            expert,
            expert,
            P(),
            gain,
            gain,
        ),
        out_specs=(
            token,
            token,
            P(),
            dense,
            dense,
            dense,
            expert,
            expert,
            expert,
            gain,
            gain,
            gain,
        ),
        check_vma=False,
    )
```

time: 642 us -> 623 us (0.970)
  waiting for transfers between devices: 190 us -> 254 us
  local copies, waits for them, and re-layouts: 72.3 us -> 46.7 us
  blocking collectives: 21.5 us -> 0 us
  Pallas kernels: 83.9 us -> 68.6 us
  starting transfers between devices: 107 us -> 95 us
  matrix products: 61.6 us -> 51.5 us
  between operations: 20.1 us -> 28.3 us
    ppermute x56 -> x48, waiting for transfers between devices: 162 us -> 194 us  [turn(): return lax.ppermute(v, CTX, pairs)]
    all_to_all x1 -> x0, blocking collectives: 21.5 us -> none  [shards(): lax.all_to_all(dense_both.reshape(8, -1, HALF_COLS), COLUMN, 0, 0, tiled=...]
    ppermute x56 -> x48, starting transfers between devices: 94.3 us -> 75.1 us  [turn(): return lax.ppermute(v, CTX, pairs)]
    all_gather x3, waiting for transfers between devices: 0.02 us -> 17 us  [the longest x1 17 us: shards(): expert_own = lax.all_gather(expert_low, DEPTH, axis=0, tiled=True)]
    pallas_call x6 -> x9, Pallas kernels: 83.9 us -> 68.6 us  [the longest x1 21.4 us: attend_back(): pl.pallas_call(functools.partial(attend_back_kernel, scale), in_specs=[in...]
    select_n x2 -> x0, other arithmetic: 11.3 us -> none  [the longest x1 7.96 us: shards(): jnp.where(first_core, expert_own, expert_other)]
    slice x26 -> x19, local copies, waits for them, and re-layouts: 21.5 us -> 12.4 us  [the longest x12 7.73 us: zero_after(): return jnp.minimum(jnp.abs(v[(0,) * v.ndim].astype(F32)), 0.0)]
    ppermute x12, waiting for transfers between devices: 1.71 us -> 10.7 us  [swap(): return lax.ppermute(v, 'core', [(0, 1), (1, 0)])]
  transfers between devices with their start and end apart: 80 -> 74, of which waited for: 38 -> 39; matrix products, arithmetic and copies ran while one was open for 25% -> 20% of each run, Pallas kernels for 10% -> 11%
where the time goes in v2:
time: 623 us; the launch traced here: 614 us
  waiting for transfers between devices  254 us (41%)
  starting transfers between devices  95 us (15%)
  other arithmetic  69.9 us (11%)
  Pallas kernels  68.6 us (11%)
  matrix products  51.5 us (8%)
  local copies, waits for them, and re-layouts  46.7 us (7%)
  between operations  28.3 us (5%)
    ppermute x48, waiting for transfers between devices, turn(): return lax.ppermute(v, CTX, pairs)  194 us
    ppermute x48, starting transfers between devices, turn(): return lax.ppermute(v, CTX, pairs)  75.1 us
    unnamed x207, local copies, waits for them, and re-layouts  26.2 us
    pallas_call x1, Pallas kernels, attend_back(): pl.pallas_call(functools.partial(attend_back_kernel, scale), in_specs=[in...  21.4 us
    dot_general x8, matrix products, dot(): return jnp.dot(left, right, preferred_element_type=F32)  18.2 us
    dot_general x6, matrix products, times_transposed(): lax.dot_general(left, right, (((1,), (1,)), ((), ())), preferred_element_...  17.8 us
    all_gather x1, waiting for transfers between devices, shards(): expert_own = lax.all_gather(expert_low, DEPTH, axis=0, tiled=True)  17 us
    dot_general x9, matrix products, transposed_times(): lax.dot_general(left, right, (((0,), (0,)), ((), ())), preferred_element_...  15.4 us
  transfers between devices with their start and end apart: 74, of which 39 were waited for; matrix products, arithmetic and copies ran while one was open for 20% of the time, Pallas kernels for 11%

profile of v2, /device:TPU:0, one launch (start us, length us, event | category | flops | bytes accessed | tf_op | source)
XLA Modules:
  0.0 613.8 jit_solution(10671500817148580769)
XLA Ops:
  11.1 5.5 all-to-all-start
  17.1 10.3 %all-to-all-done = bf16[8,12,2432]{2,1,0:T(8,128)(2,1)S(1)} async-done(((bf16[8,12,2432]{2,1,0:T(8,128)(2,1)}), bf16[8,12,2432]{2,1,0:T(8,128)(2,1)S(1)}, u32[]{:S(2)}, u32[]{:S(2)}) %all-to-all-start) | async-done | bytes 466976 | tf_op jit(solution)/shard_map/all_to_all | solution.py:652
  33.4 4.0 collective-permute-done.2
  37.5 5.8 collective-permute-done.3
  49.1 17.0 %all-gather.9.cloned.1.call-done = bf16[1,1536,1536]{2,1,0:T(8,128)(2,1)} async-done(((bf16[1,384,1536]{2,1,0:T(8,128)(2,1)}), bf16[1,1536,1536]{2,1,0:T(8,128)(2,1)}) %all-gather.9.cloned.1.call-update) | async-done | bytes 4718608 | tf_op jit(solution)/shard_map/all_gather | solution.py:665
  70.8 18.8 %collective-permute-done.6.p2 = bf16[448,2048]{1,0:T(8,128)(2,1)} collective-permute-done((bf16[448,2048]{1,0:T(8,128)(2,1)S(1)}, bf16[448,2048]{1,0:T(8,128)(2,1)}, u32[]{:S(2)}, u32[]{:S(2)}) %collective-permute-start.6) | collective-permute-done | bytes 1835040 | tf_op jit(solution)/shard_map/ppermute | solution.py:64
  89.6 5.6 shard_map.257
  109.1 4.3 collective-permute-done.10
  120.1 18.1 %collective-permute-done.13.p3 = bf16[1024,512]{1,0:T(8,128)(2,1)S(1)} collective-permute-done((bf16[1024,512]{1,0:T(8,128)(2,1)S(1)}, bf16[1024,512]{1,0:T(8,128)(2,1)S(1)}, u32[]{:S(2)}, u32[]{:S(2)}) %collective-permute-start.13) | collective-permute-done | bytes 1048608 | tf_op jit(solution)/shard_map/ppermute | solution.py:64
  157.0 18.5 %collective-permute-done.12.p2 = bf16[1024,512]{1,0:T(8,128)(2,1)} collective-permute-done((bf16[1024,512]{1,0:T(8,128)(2,1)}, bf16[1024,512]{1,0:T(8,128)(2,1)}, u32[]{:S(2)}, u32[]{:S(2)}) %collective-permute-start.12) | collective-permute-done | bytes 1048608 | tf_op jit(solution)/shard_map/ppermute | solution.py:64
  182.2 13.3 %shard_map.258 = (f32[256,768]{1,0:T(8,128)S(1)}, f32[8,256]{1,0:T(8,128)S(1)}) custom-call(s32[16]{0:T(128)S(1)} %get-tuple-element.74.chips.order_ref, s32[4]{0:T(128)S(1)} %pad_add_fusion.1.bounds, s32[8,256]{1,0:T(8,128)S(1)} %add_add_fusion.1.ranges, bf16[256,768]{1,0:T(8,128)(2,1)S(1)} %copy-done.25, bf16[1024,512]{1,0:T(8,128)(2,1)S(1)} %copy-done.18, ...), custom_call_target="tpu_custom_call" | custom-call | flops 3221225472 | bytes 8388608 | tf_op jit(solution)/shard_map/pallas_call | solution.py:303
  205.5 7.5 %collective-permute-start.24 = (bf16[512,1536]{1,0:T(8,128)(2,1)S(1)}, bf16[512,1536]{1,0:T(8,128)(2,1)}, u32[]{:S(2)}, u32[]{:S(2)}) collective-permute-start(bf16[512,1536]{1,0:T(8,128)(2,1)S(1)} %maximum_add_fusion.refs_1_), channel_id=1, source_target_pairs={{0,64},{4,20},{8,72},{12,28},{16,80},{20,4},{24,88},{28,12},{32,96... | collective-permute-start | bytes 4718600 | tf_op jit(solution)/shard_map/ppermute | solution.py:64
  216.2 3.7 collective-permute-start.27
  222.9 7.3 %collective-permute-done.27 = bf16[128,1536]{1,0:T(8,128)(2,1)S(1)} collective-permute-done((bf16[128,1536]{1,0:T(8,128)(2,1)}, bf16[128,1536]{1,0:T(8,128)(2,1)S(1)}, u32[]{:S(2)}, u32[]{:S(2)}) %collective-permute-start.27) | collective-permute-done | bytes 393248 | tf_op jit(solution)/shard_map/ppermute | solution.py:64
  230.2 6.2 %collective-permute-done.26 = bf16[128,1536]{1,0:T(8,128)(2,1)S(1)} collective-permute-done((bf16[128,1536]{1,0:T(8,128)(2,1)}, bf16[128,1536]{1,0:T(8,128)(2,1)S(1)}, u32[]{:S(2)}, u32[]{:S(2)}) %collective-permute-start.26) | collective-permute-done | bytes 393248 | tf_op jit(solution)/shard_map/ppermute | solution.py:64
  238.6 5.1 collective-permute-start.30
  248.5 4.7 shard_map.260
  263.4 6.2 %shard_map.259 = (f32[256,1536]{1,0:T(8,128)S(1)}, f32[256,1536]{1,0:T(8,128)S(1)}, bf16[6144,384]{1,0:T(8,128)(2,1)S(1)}) custom-call(bf16[256,1536]{1,0:T(8,128)(2,1)S(1)} %copy-done.16, bf16[256,1536]{1,0:T(8,128)(2,1)S(1)} %copy-done.15, bf16[6144,384]{1,0:T(8,128)(2,1)S(1)} %copy-done.20), custom_call_target="tpu_custom_call" | custom-call | flops 3623878656 | bytes 14680064 | tf_op jit(solution)/shard_map/pallas_call | solution.py:216
  274.6 7.7 %collective-permute-done.29.refs_2_ = bf16[512,1536]{1,0:T(8,128)(2,1)} collective-permute-done((bf16[512,1536]{1,0:T(8,128)(2,1)}, bf16[512,1536]{1,0:T(8,128)(2,1)}, u32[]{:S(2)}, u32[]{:S(2)}) %collective-permute-start.29) | collective-permute-done | bytes 1572896 | tf_op jit(solution)/shard_map/ppermute | solution.py:64
  282.3 5.7 shard_map.261
  296.3 4.8 fusion.12
  301.1 3.5 multiply_convert_fusion.3
  304.6 5.2 convolution_convert_fusion.2.refs_1_
  309.8 4.9 shard_map.262
  321.5 4.3 convolution_convert_fusion.1
  329.7 3.9 convolution_convert_fusion
  334.9 17.1 %collective-permute-done.32 = bf16[512,1536]{1,0:T(8,128)(2,1)S(1)} collective-permute-done((bf16[512,1536]{1,0:T(8,128)(2,1)S(1)}, bf16[512,1536]{1,0:T(8,128)(2,1)S(1)}, u32[]{:S(2)}, u32[]{:S(2)}) %collective-permute-start.32) | collective-permute-done | bytes 1572896 | tf_op jit(solution)/shard_map/ppermute | solution.py:64
  352.0 3.7 collective-permute-done.33
  359.2 5.4 collective-permute-done.35
  367.6 4.1 collective-permute-done.36
  378.6 4.1 pad_maximum_fusion.1
  386.0 7.8 %collective-permute-done.58 = bf16[1536,1536]{1,0:T(8,128)(2,1)S(1)} collective-permute-done((bf16[1536,1536]{1,0:T(8,128)(2,1)S(1)}, bf16[1536,1536]{1,0:T(8,128)(2,1)S(1)}, u32[]{:S(2)}, u32[]{:S(2)}) %collective-permute-start.58) | collective-permute-done | bytes 4718624 | tf_op jit(solution)/shard_map/ppermute | solution.py:68
  393.8 5.7 add_convert_fusion
  403.3 21.4 %shard_map.263 = (bf16[256,768]{1,0:T(8,128)(2,1)S(1)}, bf16[1024,512]{1,0:T(8,128)(2,1)S(1)}, bf16[1024,512]{1,0:T(8,128)(2,1)}, bf16[1024,512]{1,0:T(8,128)(2,1)}, bf16[1024,512]{1,0:T(8,128)(2,1)}) custom-call(s32[16]{0:T(128)S(1)} %get-tuple-element.74.chips.order_ref, s32[4]{0:T(128)S(1)} %pad_add_fusion.1.bounds, s32[8,256]{1,0:T(8,128)S(1)} %add_add_fusion.1.ranges, ...), custom_call_target="tpu_custom_call" | custom-call | flops 8053063680 | bytes 12582912 | tf_op jit(solution)/shard_map/pallas_call | solution.py:377
  435.2 12.8 %collective-permute-done.39 = bf16[1024,512]{1,0:T(8,128)(2,1)} collective-permute-done((bf16[1024,512]{1,0:T(8,128)(2,1)}, bf16[1024,512]{1,0:T(8,128)(2,1)}, u32[]{:S(2)}, u32[]{:S(2)}) %collective-permute-start.39) | collective-permute-done | bytes 1048608 | tf_op jit(solution)/shard_map/ppermute | solution.py:64
  450.5 7.3 %collective-permute-done.41 = bf16[1024,512]{1,0:T(8,128)(2,1)} collective-permute-done((bf16[1024,512]{1,0:T(8,128)(2,1)}, bf16[1024,512]{1,0:T(8,128)(2,1)}, u32[]{:S(2)}, u32[]{:S(2)}) %collective-permute-start.41) | collective-permute-done | bytes 1048608 | tf_op jit(solution)/shard_map/ppermute | solution.py:64
  481.4 6.0 shard_map.264
  492.1 10.2 %collective-permute-done.53 = bf16[384,1280]{1,0:T(8,128)(2,1)S(1)} collective-permute-done((bf16[384,1280]{1,0:T(8,128)(2,1)S(1)}, bf16[384,1280]{1,0:T(8,128)(2,1)S(1)}, u32[]{:S(2)}, u32[]{:S(2)}) %collective-permute-start.53) | collective-permute-done | bytes 983072 | tf_op jit(solution)/shard_map/ppermute | solution.py:64
  506.6 7.1 %collective-permute-done.55 = bf16[96,1280]{1,0:T(8,128)(2,1)S(1)} collective-permute-done((bf16[96,1280]{1,0:T(8,128)(2,1)S(1)}, bf16[96,1280]{1,0:T(8,128)(2,1)S(1)}, u32[]{:S(2)}, u32[]{:S(2)}) %collective-permute-start.55) | collective-permute-done | bytes 245792 | tf_op jit(solution)/shard_map/ppermute | solution.py:64
  517.5 6.8 %collective-permute-done.56 = bf16[96,1280]{1,0:T(8,128)(2,1)} collective-permute-done((bf16[96,1280]{1,0:T(8,128)(2,1)}, bf16[96,1280]{1,0:T(8,128)(2,1)}, u32[]{:S(2)}, u32[]{:S(2)}) %collective-permute-start.56) | collective-permute-done | bytes 245792 | tf_op jit(solution)/shard_map/ppermute | solution.py:64
  530.3 4.2 all-to-all-start.1
  534.5 6.9 %collective-permute-done.47 = bf16[512,1536]{1,0:T(8,128)(2,1)} collective-permute-done((bf16[512,1536]{1,0:T(8,128)(2,1)}, bf16[512,1536]{1,0:T(8,128)(2,1)}, u32[]{:S(2)}, u32[]{:S(2)}) %collective-permute-start.47) | collective-permute-done | bytes 1572896 | tf_op jit(solution)/shard_map/ppermute | solution.py:64
  541.4 4.3 add_convert_fusion.1
  559.4 8.4 %collective-permute-done.60 = f32[32,128]{1,0:T(8,128)S(1)} collective-permute-done((f32[32,128]{1,0:T(8,128)S(1)}, f32[32,128]{1,0:T(8,128)S(1)}, u32[]{:S(2)}, u32[]{:S(2)}) %collective-permute-start.60) | collective-permute-done | bytes 16416 | tf_op jit(solution)/shard_map/ppermute | solution.py:527
  572.7 3.7 collective-permute-done.62
  577.1 4.3 collective-permute-done.63
  587.8 3.8 fusion.47
  598.1 7.3 %multiply_subtract_fusion = (f32[1,384,1536]{2,1,0:T(8,128)}, f32[1,384,1536]{2,1,0:T(8,128)}, f32[1,384,1536]{2,1,0:T(8,128)}) fusion(f32[1,384,1536]{2,1,0:T(8,128)} %param.25, f32[]{:T(128)S(6)} %min.81, bf16[384,1536]{1,0:T(8,128)(2,1)S(1)} %copy-done.37, f32[1,384,1536]{2,1,0:T(8,128)} %param.26, f32[1,384,1536]{2,1,0:T(8,128)} %param.27), kind=kLoop, calls=%fused_computation.50 | loop fusion | flops 10027008 | bytes 15335428 | tf_op jit(solution)/shard_map/sub | solution.py:556
  (476 shorter events, 221.5 us)
Async XLA Ops:
  7.2 58.8 %all-gather.9.cloned.1.call-start = ((), (), s32[]{:S(2)}) async-start(), calls=%async_computation.10 | async-start | bytes 5898240 | tf_op jit(solution)/shard_map/all_gather | solution.py:665
  11.1 16.3 %all-to-all-start = ((bf16[8,12,2432]{2,1,0:T(8,128)(2,1)}), bf16[8,12,2432]{2,1,0:T(8,128)(2,1)S(1)}, u32[]{:S(2)}, u32[]{:S(2)}) async-start(bf16[8,12,2432]{2,1,0:T(8,128)(2,1)} %shard_map.256), calls=%async_computation | async-start | bytes 1245184 | tf_op jit(solution)/shard_map/all_to_all | solution.py:652
  16.6 99.5 %all-gather.5.cloned.1.call-start = ((), (), s32[]{:S(2)}) async-start(), calls=%async_computation.5 | async-start | bytes 1253376 | tf_op jit(solution)/shard_map/all_gather | solution.py:675
  29.2 14.1 %collective-permute-start.4 = (bf16[112,2048]{1,0:T(8,128)(2,1)S(1)}, bf16[112,2048]{1,0:T(8,128)(2,1)S(1)}, u32[]{:S(2)}, u32[]{:S(2)}) collective-permute-start(bf16[112,2048]{1,0:T(8,128)(2,1)S(1)} %pad_maximum_fusion.11), channel_id=1, source_target_pairs={{0,16},{4,68},{8,24},{12,76},{16,0},{20,84},{24,8},{28,92},{32,48}... | collective-permute-start | bytes 1376264 | tf_op jit(solution)/shard_map/ppermute | solution.py:64
  43.4 27.4 %collective-permute-start.7 = (bf16[448,2048]{1,0:T(8,128)(2,1)S(1)}, bf16[448,2048]{1,0:T(8,128)(2,1)}, u32[]{:S(2)}, u32[]{:S(2)}) collective-permute-start(bf16[448,2048]{1,0:T(8,128)(2,1)S(1)} %constant_dynamic-update-slice_fusion.p0), channel_id=1, source_target_pairs={{0,64},{4,20},{8,72},{12,28},{16,80},{20,4},{24,88},{28,12},{32,96... | collective-permute-start | bytes 5505032 | tf_op jit(solution)/shard_map/ppermute | solution.py:64
  46.9 42.8 %collective-permute-start.6 = (bf16[448,2048]{1,0:T(8,128)(2,1)S(1)}, bf16[448,2048]{1,0:T(8,128)(2,1)}, u32[]{:S(2)}, u32[]{:S(2)}) collective-permute-start(bf16[448,2048]{1,0:T(8,128)(2,1)S(1)} %constant_dynamic-update-slice_fusion.p0), channel_id=1, source_target_pairs={{0,96},{4,28},{8,104},{12,4},{16,112},{20,12},{24,120},{28,20},{32... | collective-permute-start | bytes 5505032 | tf_op jit(solution)/shard_map/ppermute | solution.py:64
  47.8 41.9 %collective-permute-start.5 = (bf16[448,2048]{1,0:T(8,128)(2,1)S(1)}, bf16[448,2048]{1,0:T(8,128)(2,1)}, u32[]{:S(2)}, u32[]{:S(2)}) collective-permute-start(bf16[448,2048]{1,0:T(8,128)(2,1)S(1)} %constant_dynamic-update-slice_fusion.p0), channel_id=1, source_target_pairs={{0,32},{4,12},{8,40},{12,20},{16,48},{20,28},{24,56},{28,4},{32,64... | collective-permute-start | bytes 5505032 | tf_op jit(solution)/shard_map/ppermute | solution.py:64
  68.6 190.3 %all-gather.7.cloned.1.call-start = ((), (), s32[]{:S(2)}) async-start(), calls=%async_computation.6 | async-start | bytes 5898240 | tf_op jit(solution)/shard_map/all_gather | solution.py:676
  113.4 24.9 %collective-permute-start.13 = (bf16[1024,512]{1,0:T(8,128)(2,1)S(1)}, bf16[1024,512]{1,0:T(8,128)(2,1)S(1)}, u32[]{:S(2)}, u32[]{:S(2)}) collective-permute-start(bf16[1024,512]{1,0:T(8,128)(2,1)S(1)} %constant_dynamic-update-slice_fusion.5.p0), channel_id=1, source_target_pairs={{0,64},{4,20},{8,72},{12,28},{16,80},{20,4},{24,88},{28,12},{32,96... | collective-permute-start | bytes 3145736 | tf_op jit(solution)/shard_map/ppermute | solution.py:64
  116.1 262.4 %reduce-scatter.4.cloned.1.call-start = ((), (), s32[]{:S(2)}) async-start(), calls=%async_computation.7 | async-start | bytes 5898240 | tf_op jit(solution)/shard_map/reduce_scatter | solution.py:724
  116.2 24.2 %collective-permute-start.16 = (bf16[128,1536]{1,0:T(8,128)(2,1)}, bf16[128,1536]{1,0:T(8,128)(2,1)S(1)}, u32[]{:S(2)}, u32[]{:S(2)}) collective-permute-start(bf16[128,1536]{1,0:T(8,128)(2,1)} %bitcast.10), channel_id=1, source_target_pairs={{0,16},{4,68},{8,24},{12,76},{16,0},{20,84},{24,8},{28,92},{32,48}... | collective-permute-start | bytes 1179656 | tf_op jit(solution)/shard_map/ppermute | solution.py:64
  117.7 22.8 %collective-permute-start.15 = (bf16[128,1536]{1,0:T(8,128)(2,1)}, bf16[128,1536]{1,0:T(8,128)(2,1)S(1)}, u32[]{:S(2)}, u32[]{:S(2)}) collective-permute-start(bf16[128,1536]{1,0:T(8,128)(2,1)} %bitcast.10), channel_id=1, source_target_pairs={{0,24},{4,100},{8,0},{12,108},{16,8},{20,116},{24,16},{28,124},{32... | collective-permute-start | bytes 1179656 | tf_op jit(solution)/shard_map/ppermute | solution.py:64
  120.0 20.4 %collective-permute-start.14 = (bf16[128,1536]{1,0:T(8,128)(2,1)}, bf16[128,1536]{1,0:T(8,128)(2,1)S(1)}, u32[]{:S(2)}, u32[]{:S(2)}) collective-permute-start(bf16[128,1536]{1,0:T(8,128)(2,1)} %bitcast.10), channel_id=1, source_target_pairs={{0,8},{4,36},{8,16},{12,44},{16,24},{20,52},{24,0},{28,60},{32,40}... | collective-permute-start | bytes 1179656 | tf_op jit(solution)/shard_map/ppermute | solution.py:64
  120.0 82.6 %collective-permute-start.21 = (bf16[128,1536]{1,0:T(8,128)(2,1)}, bf16[128,1536]{1,0:T(8,128)(2,1)}, u32[]{:S(2)}, u32[]{:S(2)}) collective-permute-start(bf16[128,1536]{1,0:T(8,128)(2,1)} %bitcast.10), channel_id=1, source_target_pairs={{0,4},{4,0},{1,5},{5,1},{2,6},{6,2},{3,7},{7,3},{8,12},{12,8},{9,1... | collective-permute-start | bytes 1179656 | tf_op jit(solution)/shard_map/ppermute | solution.py:68
  143.7 51.9 %collective-permute-start.18 = (bf16[512,1536]{1,0:T(8,128)(2,1)S(1)}, bf16[512,1536]{1,0:T(8,128)(2,1)S(1)}, u32[]{:S(2)}, u32[]{:S(2)}) collective-permute-start(bf16[512,1536]{1,0:T(8,128)(2,1)S(1)} %maximum_add_fusion.refs_1_), channel_id=1, source_target_pairs={{0,96},{4,28},{8,104},{12,4},{16,112},{20,12},{24,120},{28,20},{32... | collective-permute-start | bytes 4718600 | tf_op jit(solution)/shard_map/ppermute | solution.py:64
  145.8 51.0 %collective-permute-start.17 = (bf16[512,1536]{1,0:T(8,128)(2,1)S(1)}, bf16[512,1536]{1,0:T(8,128)(2,1)}, u32[]{:S(2)}, u32[]{:S(2)}) collective-permute-start(bf16[512,1536]{1,0:T(8,128)(2,1)S(1)} %maximum_add_fusion.refs_1_), channel_id=1, source_target_pairs={{0,32},{4,12},{8,40},{12,20},{16,48},{20,28},{24,56},{28,4},{32,64... | collective-permute-start | bytes 4718600 | tf_op jit(solution)/shard_map/ppermute | solution.py:64
  145.8 29.7 %collective-permute-start.12 = (bf16[1024,512]{1,0:T(8,128)(2,1)}, bf16[1024,512]{1,0:T(8,128)(2,1)}, u32[]{:S(2)}, u32[]{:S(2)}) collective-permute-start(bf16[1024,512]{1,0:T(8,128)(2,1)} %copy-done.17), channel_id=1, source_target_pairs={{0,96},{4,28},{8,104},{12,4},{16,112},{20,12},{24,120},{28,20},{32... | collective-permute-start | bytes 3145736 | tf_op jit(solution)/shard_map/ppermute | solution.py:64
  149.1 29.7 %collective-permute-start.11 = (bf16[1024,512]{1,0:T(8,128)(2,1)}, bf16[1024,512]{1,0:T(8,128)(2,1)}, u32[]{:S(2)}, u32[]{:S(2)}) collective-permute-start(bf16[1024,512]{1,0:T(8,128)(2,1)} %copy-done.17), channel_id=1, source_target_pairs={{0,32},{4,12},{8,40},{12,20},{16,48},{20,28},{24,56},{28,4},{32,64... | collective-permute-start | bytes 3145736 | tf_op jit(solution)/shard_map/ppermute | solution.py:64
  205.5 41.6 %collective-permute-start.24 = (bf16[512,1536]{1,0:T(8,128)(2,1)S(1)}, bf16[512,1536]{1,0:T(8,128)(2,1)}, u32[]{:S(2)}, u32[]{:S(2)}) collective-permute-start(bf16[512,1536]{1,0:T(8,128)(2,1)S(1)} %maximum_add_fusion.refs_1_), channel_id=1, source_target_pairs={{0,64},{4,20},{8,72},{12,28},{16,80},{20,4},{24,88},{28,12},{32,96... | collective-permute-start | bytes 4718600 | tf_op jit(solution)/shard_map/ppermute | solution.py:64
  214.4 81.8 %collective-permute-start.31 = (bf16[1536,1536]{1,0:T(8,128)(2,1)}, bf16[1536,1536]{1,0:T(8,128)(2,1)}, u32[]{:S(2)}, u32[]{:S(2)}) collective-permute-start(bf16[1536,1536]{1,0:T(8,128)(2,1)} %bitcast.133), channel_id=1, source_target_pairs={{0,4},{4,0},{1,5},{5,1},{2,6},{6,2},{3,7},{7,3},{8,12},{12,8},{9,1... | collective-permute-start | bytes 14155784 | tf_op jit(solution)/shard_map/ppermute | solution.py:68
  216.2 14.0 %collective-permute-start.27 = (bf16[128,1536]{1,0:T(8,128)(2,1)}, bf16[128,1536]{1,0:T(8,128)(2,1)S(1)}, u32[]{:S(2)}, u32[]{:S(2)}) collective-permute-start(bf16[128,1536]{1,0:T(8,128)(2,1)} %multiply_convert_fusion.6), channel_id=1, source_target_pairs={{0,16},{4,68},{8,24},{12,76},{16,0},{20,84},{24,8},{28,92},{32,48}... | collective-permute-start | bytes 1179656 | tf_op jit(solution)/shard_map/ppermute | solution.py:64
  219.8 16.5 %collective-permute-start.26 = (bf16[128,1536]{1,0:T(8,128)(2,1)}, bf16[128,1536]{1,0:T(8,128)(2,1)S(1)}, u32[]{:S(2)}, u32[]{:S(2)}) collective-permute-start(bf16[128,1536]{1,0:T(8,128)(2,1)} %multiply_convert_fusion.6), channel_id=1, source_target_pairs={{0,24},{4,100},{8,0},{12,108},{16,8},{20,116},{24,16},{28,124},{32... | collective-permute-start | bytes 1179656 | tf_op jit(solution)/shard_map/ppermute | solution.py:64
  220.7 15.7 %collective-permute-start.25 = (bf16[128,1536]{1,0:T(8,128)(2,1)}, bf16[128,1536]{1,0:T(8,128)(2,1)S(1)}, u32[]{:S(2)}, u32[]{:S(2)}) collective-permute-start(bf16[128,1536]{1,0:T(8,128)(2,1)} %multiply_convert_fusion.6), channel_id=1, source_target_pairs={{0,8},{4,36},{8,16},{12,44},{16,24},{20,52},{24,0},{28,60},{32,40}... | collective-permute-start | bytes 1179656 | tf_op jit(solution)/shard_map/ppermute | solution.py:64
  238.6 36.0 %collective-permute-start.30 = (bf16[512,1536]{1,0:T(8,128)(2,1)}, bf16[512,1536]{1,0:T(8,128)(2,1)}, u32[]{:S(2)}, u32[]{:S(2)}) collective-permute-start(bf16[512,1536]{1,0:T(8,128)(2,1)} %pad_maximum_fusion.2.refs_0_), channel_id=1, source_target_pairs={{0,64},{4,20},{8,72},{12,28},{16,80},{20,4},{24,88},{28,12},{32,96... | collective-permute-start | bytes 4718600 | tf_op jit(solution)/shard_map/ppermute | solution.py:64
  243.7 38.6 %collective-permute-start.29 = (bf16[512,1536]{1,0:T(8,128)(2,1)}, bf16[512,1536]{1,0:T(8,128)(2,1)}, u32[]{:S(2)}, u32[]{:S(2)}) collective-permute-start(bf16[512,1536]{1,0:T(8,128)(2,1)} %pad_maximum_fusion.2.refs_0_), channel_id=1, source_target_pairs={{0,96},{4,28},{8,104},{12,4},{16,112},{20,12},{24,120},{28,20},{32... | collective-permute-start | bytes 4718600 | tf_op jit(solution)/shard_map/ppermute | solution.py:64
  245.8 36.5 %collective-permute-start.28 = (bf16[512,1536]{1,0:T(8,128)(2,1)}, bf16[512,1536]{1,0:T(8,128)(2,1)}, u32[]{:S(2)}, u32[]{:S(2)}) collective-permute-start(bf16[512,1536]{1,0:T(8,128)(2,1)} %pad_maximum_fusion.2.refs_0_), channel_id=1, source_target_pairs={{0,32},{4,12},{8,40},{12,20},{16,48},{20,28},{24,56},{28,4},{32,64... | collective-permute-start | bytes 4718600 | tf_op jit(solution)/shard_map/ppermute | solution.py:64
  274.2 252.3 %reduce-scatter.6.cloned.1.call-start = ((), (), s32[]{:S(2)}) async-start(), calls=%async_computation.8 | async-start | bytes 3760128 | tf_op jit(solution)/shard_map/reduce_scatter | solution.py:776
  274.3 84.9 %collective-permute-start.23 = (f32[128,1536]{1,0:T(8,128)S(1)}, f32[128,1536]{1,0:T(8,128)S(1)}, u32[]{:S(2)}, u32[]{:S(2)}) collective-permute-start(f32[128,1536]{1,0:T(8,128)S(1)} %constant_dynamic-slice_fusion.3), channel_id=1, source_target_pairs={{0,4},{4,0},{1,5},{5,1},{2,6},{6,2},{3,7},{7,3},{8,12},{12,8},{9,1... | collective-permute-start | bytes 2359304 | tf_op jit(solution)/shard_map/ppermute | solution.py:68
  314.7 37.3 %collective-permute-start.32 = (bf16[512,1536]{1,0:T(8,128)(2,1)S(1)}, bf16[512,1536]{1,0:T(8,128)(2,1)S(1)}, u32[]{:S(2)}, u32[]{:S(2)}) collective-permute-start(bf16[512,1536]{1,0:T(8,128)(2,1)S(1)} %get-tuple-element.42), channel_id=1, source_target_pairs={{0,96},{4,28},{8,104},{12,4},{16,112},{20,12},{24,120},{28,20},{32... | collective-permute-start | bytes 4718600 | tf_op jit(solution)/shard_map/ppermute | solution.py:64
  317.2 38.5 %collective-permute-start.33 = (bf16[512,1536]{1,0:T(8,128)(2,1)S(1)}, bf16[512,1536]{1,0:T(8,128)(2,1)S(1)}, u32[]{:S(2)}, u32[]{:S(2)}) collective-permute-start(bf16[512,1536]{1,0:T(8,128)(2,1)S(1)} %get-tuple-element.43), channel_id=1, source_target_pairs={{0,32},{4,12},{8,40},{12,20},{16,48},{20,28},{24,56},{28,4},{32,64... | collective-permute-start | bytes 4718600 | tf_op jit(solution)/shard_map/ppermute | solution.py:64
  317.2 38.5 %collective-permute-start.34 = (bf16[512,1536]{1,0:T(8,128)(2,1)S(1)}, bf16[512,1536]{1,0:T(8,128)(2,1)S(1)}, u32[]{:S(2)}, u32[]{:S(2)}) collective-permute-start(bf16[512,1536]{1,0:T(8,128)(2,1)S(1)} %get-tuple-element.44), channel_id=1, source_target_pairs={{0,64},{4,20},{8,72},{12,28},{16,80},{20,4},{24,88},{28,12},{32,96... | collective-permute-start | bytes 4718600 | tf_op jit(solution)/shard_map/ppermute | solution.py:64
  358.6 13.2 %collective-permute-start.36 = (bf16[128,1536]{1,0:T(8,128)(2,1)S(1)}, bf16[128,1536]{1,0:T(8,128)(2,1)S(1)}, u32[]{:S(2)}, u32[]{:S(2)}) collective-permute-start(bf16[128,1536]{1,0:T(8,128)(2,1)S(1)} %get-tuple-element.92), channel_id=1, source_target_pairs={{0,8},{4,36},{8,16},{12,44},{16,24},{20,52},{24,0},{28,60},{32,40}... | collective-permute-start | bytes 1179656 | tf_op jit(solution)/shard_map/ppermute | solution.py:64
  382.7 163.0 %reduce-scatter.8.cloned.1.call-start = ((), (), s32[]{:S(2)}) async-start(), calls=%async_computation.9 | async-start | bytes 5898240 | tf_op jit(solution)/shard_map/reduce_scatter | solution.py:752
  425.4 22.7 %collective-permute-start.39 = (bf16[1024,512]{1,0:T(8,128)(2,1)}, bf16[1024,512]{1,0:T(8,128)(2,1)}, u32[]{:S(2)}, u32[]{:S(2)}) collective-permute-start(bf16[1024,512]{1,0:T(8,128)(2,1)} %get-tuple-element.47), channel_id=1, source_target_pairs={{0,96},{4,28},{8,104},{12,4},{16,112},{20,12},{24,120},{28,20},{32... | collective-permute-start | bytes 3145736 | tf_op jit(solution)/shard_map/ppermute | solution.py:64
  427.8 22.7 %collective-permute-start.40 = (bf16[1024,512]{1,0:T(8,128)(2,1)}, bf16[1024,512]{1,0:T(8,128)(2,1)}, u32[]{:S(2)}, u32[]{:S(2)}) collective-permute-start(bf16[1024,512]{1,0:T(8,128)(2,1)} %get-tuple-element.48), channel_id=1, source_target_pairs={{0,32},{4,12},{8,40},{12,20},{16,48},{20,28},{24,56},{28,4},{32,64... | collective-permute-start | bytes 3145736 | tf_op jit(solution)/shard_map/ppermute | solution.py:64
  427.8 30.0 %collective-permute-start.41 = (bf16[1024,512]{1,0:T(8,128)(2,1)}, bf16[1024,512]{1,0:T(8,128)(2,1)}, u32[]{:S(2)}, u32[]{:S(2)}) collective-permute-start(bf16[1024,512]{1,0:T(8,128)(2,1)} %get-tuple-element.49), channel_id=1, source_target_pairs={{0,64},{4,20},{8,72},{12,28},{16,80},{20,4},{24,88},{28,12},{32,96... | collective-permute-start | bytes 3145736 | tf_op jit(solution)/shard_map/ppermute | solution.py:64
  476.1 15.8 %collective-permute-start.54 = (bf16[384,1280]{1,0:T(8,128)(2,1)S(1)}, bf16[384,1280]{1,0:T(8,128)(2,1)S(1)}, u32[]{:S(2)}, u32[]{:S(2)}) collective-permute-start(bf16[384,1280]{1,0:T(8,128)(2,1)S(1)} %convolution_convert_fusion.9), channel_id=1, source_target_pairs={{0,64},{4,20},{8,72},{12,28},{16,80},{20,4},{24,88},{28,12},{32,96... | collective-permute-start | bytes 2949128 | tf_op jit(solution)/shard_map/ppermute | solution.py:64
  477.5 24.8 %collective-permute-start.53 = (bf16[384,1280]{1,0:T(8,128)(2,1)S(1)}, bf16[384,1280]{1,0:T(8,128)(2,1)S(1)}, u32[]{:S(2)}, u32[]{:S(2)}) collective-permute-start(bf16[384,1280]{1,0:T(8,128)(2,1)S(1)} %convolution_convert_fusion.10), channel_id=1, source_target_pairs={{0,32},{4,12},{8,40},{12,20},{16,48},{20,28},{24,56},{28,4},{32,64... | collective-permute-start | bytes 2949128 | tf_op jit(solution)/shard_map/ppermute | solution.py:64
  478.7 24.5 %collective-permute-start.52 = (bf16[384,1280]{1,0:T(8,128)(2,1)S(1)}, bf16[384,1280]{1,0:T(8,128)(2,1)S(1)}, u32[]{:S(2)}, u32[]{:S(2)}) collective-permute-start(bf16[384,1280]{1,0:T(8,128)(2,1)S(1)} %convolution_convert_fusion.11), channel_id=1, source_target_pairs={{0,96},{4,28},{8,104},{12,4},{16,112},{20,12},{24,120},{28,20},{32... | collective-permute-start | bytes 2949128 | tf_op jit(solution)/shard_map/ppermute | solution.py:64
  489.9 16.5 %collective-permute-start.51 = (f32[128,1536]{1,0:T(8,128)S(1)}, f32[128,1536]{1,0:T(8,128)S(1)}, u32[]{:S(2)}, u32[]{:S(2)}) collective-permute-start(f32[128,1536]{1,0:T(8,128)S(1)} %constant_dynamic-slice_fusion.2), channel_id=1, source_target_pairs={{0,4},{4,0},{1,5},{5,1},{2,6},{6,2},{3,7},{7,3},{8,12},{12,8},{9,1... | collective-permute-start | bytes 2359304 | tf_op jit(solution)/shard_map/ppermute | solution.py:68
  490.0 44.5 %collective-permute-start.45 = (bf16[512,1536]{1,0:T(8,128)(2,1)}, bf16[512,1536]{1,0:T(8,128)(2,1)}, u32[]{:S(2)}, u32[]{:S(2)}) collective-permute-start(bf16[512,1536]{1,0:T(8,128)(2,1)} %get-tuple-element.51), channel_id=1, source_target_pairs={{0,96},{4,28},{8,104},{12,4},{16,112},{20,12},{24,120},{28,20},{32... | collective-permute-start | bytes 4718600 | tf_op jit(solution)/shard_map/ppermute | solution.py:64
  491.9 42.6 %collective-permute-start.46 = (bf16[512,1536]{1,0:T(8,128)(2,1)}, bf16[512,1536]{1,0:T(8,128)(2,1)}, u32[]{:S(2)}, u32[]{:S(2)}) collective-permute-start(bf16[512,1536]{1,0:T(8,128)(2,1)} %get-tuple-element.52), channel_id=1, source_target_pairs={{0,32},{4,12},{8,40},{12,20},{16,48},{20,28},{24,56},{28,4},{32,64... | collective-permute-start | bytes 4718600 | tf_op jit(solution)/shard_map/ppermute | solution.py:64
  502.3 39.1 %collective-permute-start.47 = (bf16[512,1536]{1,0:T(8,128)(2,1)}, bf16[512,1536]{1,0:T(8,128)(2,1)}, u32[]{:S(2)}, u32[]{:S(2)}) collective-permute-start(bf16[512,1536]{1,0:T(8,128)(2,1)} %get-tuple-element.53), channel_id=1, source_target_pairs={{0,64},{4,20},{8,72},{12,28},{16,80},{20,4},{24,88},{28,12},{32,96... | collective-permute-start | bytes 4718600 | tf_op jit(solution)/shard_map/ppermute | solution.py:64
  517.5 70.2 %collective-permute-start.22 = (f32[128,1536]{1,0:T(8,128)}, f32[128,1536]{1,0:T(8,128)}, u32[]{:S(2)}, u32[]{:S(2)}) collective-permute-start(f32[128,1536]{1,0:T(8,128)} %constant_dynamic-slice_fusion.4), channel_id=1, source_target_pairs={{0,4},{4,0},{1,5},{5,1},{2,6},{6,2},{3,7},{7,3},{8,12},{12,8},{9,1... | collective-permute-start | bytes 2359304 | tf_op jit(solution)/shard_map/ppermute | solution.py:68
  530.3 17.9 %all-to-all-start.1 = ((bf16[8,12,2432]{2,1,0:T(8,128)(2,1)}), bf16[8,12,2432]{2,1,0:T(8,128)(2,1)}, u32[]{:S(2)}, u32[]{:S(2)}) async-start(bf16[8,12,2432]{2,1,0:T(8,128)(2,1)} %reshape.316), calls=%async_computation.3 | async-start | bytes 1245184 | tf_op jit(solution)/shard_map/all_to_all | solution.py:789
  555.2 32.5 %collective-permute-start.48 = (bf16[128,1536]{1,0:T(8,128)(2,1)}, bf16[128,1536]{1,0:T(8,128)(2,1)}, u32[]{:S(2)}, u32[]{:S(2)}) collective-permute-start(bf16[128,1536]{1,0:T(8,128)(2,1)} %get-tuple-element.87), channel_id=1, source_target_pairs={{0,24},{4,100},{8,0},{12,108},{16,8},{20,116},{24,16},{28,124},{32... | collective-permute-start | bytes 1179656 | tf_op jit(solution)/shard_map/ppermute | solution.py:64
  555.9 31.8 %collective-permute-start.50 = (bf16[128,1536]{1,0:T(8,128)(2,1)}, bf16[128,1536]{1,0:T(8,128)(2,1)}, u32[]{:S(2)}, u32[]{:S(2)}) collective-permute-start(bf16[128,1536]{1,0:T(8,128)(2,1)} %get-tuple-element.88), channel_id=1, source_target_pairs={{0,16},{4,68},{8,24},{12,76},{16,0},{20,84},{24,8},{28,92},{32,48}... | collective-permute-start | bytes 1179656 | tf_op jit(solution)/shard_map/ppermute | solution.py:64
  555.9 31.9 %collective-permute-start.49 = (bf16[128,1536]{1,0:T(8,128)(2,1)}, bf16[128,1536]{1,0:T(8,128)(2,1)}, u32[]{:S(2)}, u32[]{:S(2)}) collective-permute-start(bf16[128,1536]{1,0:T(8,128)(2,1)} %get-tuple-element.89), channel_id=1, source_target_pairs={{0,8},{4,36},{8,16},{12,44},{16,24},{20,52},{24,0},{28,60},{32,40}... | collective-permute-start | bytes 1179656 | tf_op jit(solution)/shard_map/ppermute | solution.py:64
  (110 other events, 1153.9 us)
Sparse Core Ops, SparseCore 0:
  10.3 55.7 all-gather.8
  68.7 44.4 all-gather.4
  116.3 62.0 all-gather.6
  274.3 49.1 reduce-scatter.3
  382.8 79.4 reduce-scatter.5
  464.6 48.9 reduce-scatter.7
